TPU v7x, 128 devices: a whole 4x4x4 slice. The times are simulated.
128 devices in a mesh: row: 8 (over z, core), col: 16 (over y, x).
Axes of the slice: x: 4, y: 4, z: 4, core: 2. Of those that a mesh axis runs over, the one named last changes fastest.
Arguments:
- fem_basis: float32 [2, 16, 2, 262144], P(None, None, None, ('row', 'col')), may hold values from -8 to 8
- bem_basis: float32 [2, 16, 2, 16384], P(None, None, None, ('row', 'col')), may hold values from -8 to 8
- fem_diagonal: float32 [262144], P(('row', 'col')), may hold values from 1 to 4
- fem_values: float32 [16, 262144], P(None, ('row', 'col')), may hold values from -1.5 to 1.5
- fem_columns: int32 [16, 262144], P(None, ('row', 'col')), may hold values from 0 to 2559
- halo_rows: int32 [4, 16384], P(None, ('row', 'col')), may hold values from 0 to 2047
- bem_matrix: bfloat16 [2, 16384, 16384], P(None, 'row', 'col'), may hold values from -0.03125 to 0.03125
- trace_rows: int32 [32768], P(('row', 'col')), may hold values from -1 to 2047, as said below
- bem_slot: int32 [16384], P(('row', 'col')), may hold values from 0 to 255, as said below
Outputs:
- next_fem: float32 [16, 2, 262144], P(None, None, ('row', 'col'))
- next_bem: float32 [16, 2, 16384], P(None, None, ('row', 'col'))
- hessenberg: float32 [2, 16, 16], replicated
- r_factor: float32 [16, 16], replicated
Inputs may be any that keep to these rules, and one draw needn't show every extreme that they name: `trace_rows`: each device's entries form one block of 2 slots per BEM owner, owners in row+col order; a block is all -1 (unused) or holds local FEM rows, the rows of one device being distinct; every owner is fed by exactly 64 full blocks. `bem_slot`: value = source device along row+col times 2 plus slot; within one owner the values are distinct and are exactly the full slots that trace_rows sends to that owner.
All inputs are finite; a program needn't handle non-finite values.
Results may differ from a plain program's by a relative error of at most 0.0014.
Values may be sent and summed in bfloat16 or wider, within the bound.
A program may use at most 128 MiB of HBM per device.

v0:
```python
import functools

import jax
import jax.numpy as jnp
from jax import lax
from jax.sharding import Mesh
from jax.sharding import PartitionSpec as P

COL = ("col_0", "col_1")
ROW = ("row_0", "row_1")
ROW_COL = ("row_0", "row_1", "col_0", "col_1")


HIGHEST = lax.Precision.HIGHEST


def passed_along(shard, axis, by):
    peers = lax.axis_size(axis)
    pairs = [(i, i + by) for i in range(peers) if 0 <= i + by < peers]
    return lax.ppermute(shard, axis, pairs)


def from_everyone(shard, axis):
    peers = lax.axis_size(axis)
    return lax.all_to_all(
        jnp.broadcast_to(shard[None], (peers, *shard.shape)), axis, 0, 0, tiled=True
    )


def joined_along(pieces, dim):
    dims = list(pieces.shape[1:])
    dims[dim] *= pieces.shape[0]
    return jnp.moveaxis(pieces, 0, dim).reshape(dims)


def gather_directly(shard, axis, dim):
    pieces = from_everyone(shard, axis)
    return joined_along(pieces, dim)


def cut_along(shard, dim, peers):
    before, after = (shard.shape[:dim], shard.shape[dim + 1 :])
    return jnp.moveaxis(shard.reshape(*before, peers, -1, *after), dim, 0)


def sent_and_summed(shard, axis, dim):
    peers = lax.axis_size(axis)
    pieces = lax.all_to_all(cut_along(shard, dim, peers), axis, 0, 0, tiled=True)
    return jnp.sum(pieces, axis=0)


def sent_together(arrays, axis, split_dim, concat_dim, along):
    widths = [a.shape[along] for a in arrays]
    both = jnp.concatenate(arrays, axis=along)
    filled = lax.all_to_all(both, axis, split_axis=split_dim, concat_axis=concat_dim, tiled=True)
    return tuple(jnp.split(filled, [sum(widths[:k]) for k in range(1, len(widths))], axis=along))


def one_axis_at_a_time(shard, axes):
    return functools.reduce(lax.psum, axes, shard)


def dotted(lefts, rights):
    return lax.dot_general(
        lefts.reshape(lefts.shape[0], -1),
        rights.reshape(rights.shape[0], -1),
        (((1,), (1,)), ((), ())),
        precision=HIGHEST,
        preferred_element_type=jnp.float32,
    )


def combine(coeffs, basis):
    flat_basis = basis.reshape(basis.shape[0], -1)
    merged = lax.dot_general(
        coeffs,
        flat_basis,
        (((0,), (0,)), ((), ())),
        precision=HIGHEST,
        preferred_element_type=jnp.float32,
    )
    return merged.reshape((coeffs.shape[1],) + basis.shape[1:])


def exterior(vectors, halo_rows):
    outbound = jnp.take(vectors, halo_rows, axis=2)
    from_left = passed_along(outbound[:, :, 0], COL, 1)
    from_right = passed_along(outbound[:, :, 1], COL, -1)
    from_above = passed_along(outbound[:, :, 2], ROW, 1)
    from_below = passed_along(outbound[:, :, 3], ROW, -1)
    return jnp.concatenate([vectors, from_left, from_right, from_above, from_below], axis=2)


def fem_product(vectors, fem_diagonal, fem_values, fem_columns, halo_rows):
    extended = exterior(vectors, halo_rows)
    gathered = jnp.take(extended, fem_columns, axis=2)
    return fem_diagonal * vectors + jnp.sum(fem_values * gathered, axis=2)


def bem_product(vectors, bem_matrix):
    rounded = vectors.astype(jnp.bfloat16)
    portion = gather_directly(rounded, ROW, 2)
    flat_part = portion.reshape(-1, portion.shape[-1])
    products = lax.dot_general(
        flat_part, bem_matrix, (((1,), (2,)), ((), ())), preferred_element_type=jnp.float32
    )
    products = products.reshape(rounded.shape[0], 2, 2, -1)
    real_part = products[:, 0, 0] - products[:, 1, 1]
    imag_part = products[:, 0, 1] + products[:, 1, 0]
    partial_rows = jnp.stack([real_part, imag_part], axis=1)
    return sent_and_summed(partial_rows, COL, 2)


def body(
    fem_basis,
    bem_basis,
    fem_diagonal,
    fem_values,
    fem_columns,
    halo_rows,
    bem_matrix,
    trace_rows,
    bem_slot,
):
    blocks = fem_basis.shape[0]
    rhs_count = fem_basis.shape[1]
    fem_last = fem_basis[blocks - 1]
    bem_last = bem_basis[blocks - 1]
    fem_image = fem_product(fem_last, fem_diagonal, fem_values, fem_columns, halo_rows)
    bem_image = bem_product(bem_last, bem_matrix)
    active = trace_rows >= 0
    clipped = jnp.where(active, trace_rows, 0)
    mask_row = active.astype(jnp.float32)
    outgoing = jnp.take(fem_last, clipped, axis=2) * mask_row
    slot_count = trace_rows.shape[0]
    selector = (bem_slot[:, None] == jnp.arange(slot_count, dtype=jnp.int32)[None, :]).astype(
        jnp.float32
    )
    returning = lax.dot_general(
        bem_last,
        selector,
        (((2,), (0,)), ((), ())),
        precision=HIGHEST,
        preferred_element_type=jnp.float32,
    )
    arriving, answers = sent_together((outgoing, returning), ROW_COL, 2, 2, 0)
    fem_image = fem_image.at[:, :, clipped].add(answers * mask_row)
    bem_image = bem_image + lax.dot_general(
        arriving,
        selector,
        (((2,), (1,)), ((), ())),
        precision=HIGHEST,
        preferred_element_type=jnp.float32,
    )
    device_count = lax.axis_size(ROW) * lax.axis_size(COL)
    count = 2.0 * device_count * (fem_last.shape[2] + bem_last.shape[2])
    fem_flat = fem_basis.reshape(blocks * rhs_count, 2, -1)
    bem_flat = bem_basis.reshape(blocks * rhs_count, 2, -1)
    coeffs_one = (
        one_axis_at_a_time(dotted(fem_flat, fem_image) + dotted(bem_flat, bem_image), ROW_COL)
        / count
    )
    fem_once = fem_image - combine(coeffs_one, fem_flat)
    bem_once = bem_image - combine(coeffs_one, bem_flat)
    coeffs_two = (
        one_axis_at_a_time(dotted(fem_flat, fem_once) + dotted(bem_flat, bem_once), ROW_COL) / count
    )
    fem_twice = fem_once - combine(coeffs_two, fem_flat)
    bem_twice = bem_once - combine(coeffs_two, bem_flat)
    gram_matrix = (
        one_axis_at_a_time(dotted(fem_twice, fem_twice) + dotted(bem_twice, bem_twice), ROW_COL)
        / count
    )
    lower_factor = jnp.linalg.cholesky(gram_matrix)
    inverse_lower = jax.scipy.linalg.solve_triangular(
        lower_factor, jnp.eye(rhs_count, dtype=jnp.float32), lower=True
    )
    next_fem = combine(inverse_lower.T, fem_twice)
    next_bem = combine(inverse_lower.T, bem_twice)
    hessenberg = (coeffs_one + coeffs_two).reshape(blocks, rhs_count, rhs_count)
    return (next_fem, next_bem, hessenberg, lower_factor.T)


def solution(mesh):
    finer = Mesh(mesh.devices.reshape(4, 2, 4, 4), ("row_0", "row_1", "col_0", "col_1"))
    return jax.shard_map(
        body,
        mesh=finer,
        in_specs=(
            P(None, None, None, ROW_COL),
            P(None, None, None, ROW_COL),
            P(ROW_COL),
            P(None, ROW_COL),
            P(None, ROW_COL),
            P(None, ROW_COL),
            P(None, ROW, COL),
            P(ROW_COL),
            P(ROW_COL),
        ),
        out_specs=(P(None, None, ROW_COL), P(None, None, ROW_COL), P(), P()),
        check_vma=False,
    )
```

profile of v0, /device:TPU:1, one launch (start us, length us, event | category | flops | bytes accessed | tf_op | source)
XLA Modules:
  0.0 499.7 jit_solution(1784777082215200466)
XLA Ops:
  4.7 2.1 gather_fusion
  8.4 4.6 collective-permute-start
  14.3 4.4 collective-permute-start.2
  21.3 5.5 %all-to-all-start.1 = ((bf16[8,16,2,128]{3,1,2,0:T(8,128)(2,1)}), bf16[8,16,2,128]{3,1,2,0:T(8,128)(2,1)S(1)}, u32[]{:S(2)}, u32[]{:S(2)}) async-start(bf16[8,16,2,128]{3,1,2,0:T(8,128)(2,1)} %broadcast_in_dim.65), calls=%async_computation.1 | async-start | bytes 131072 | tf_op jit(solution)/shard_map/all_to_all | solution.py:25
  37.4 224.2 %gather_fusion.1 = f32[32768,16,2]{1,2,0:T(2,128)} fusion(f32[16,2,2560]{0,1,2:T(2,128)} %constant_dynamic-update-slice_fusion, s32[32768]{0:T(1024)S(1)} %broadcast_clamp_fusion), kind=kCustom, calls=%fused_computation.1 | custom fusion | bytes 8519680 | tf_op jit(solution)/shard_map/jit(_take)/gather | solution.py:96
  261.6 77.4 %multiply_reduce_fusion = f32[2048,16,2]{1,2,0:T(2,128)S(1)} fusion(f32[16,2048,16,2]{2,3,1,0:T(2,128)} %bitcast.203, pred[16,2048]{1,0:T(8,128)(4,1)S(1)} %compare_and_fusion, f32[16,2048]{1,0:T(8,128)S(1)} %copy-done.5), kind=kLoop, calls=%fused_computation.4 | loop fusion | flops 3080192 | bytes 4620288 | tf_op jit(solution)/shard_map/reduce_sum | solution.py:97
  339.0 6.6 %bitcast_add_fusion = f32[16,2,2048]{0,1,2:T(2,128)} fusion(f32[2048,16,2]{1,2,0:T(2,128)S(1)} %multiply_reduce_fusion, f32[2048]{0:T(1024)S(1)} %copy-done.6, f32[1,16,2,2048]{1,2,3,0:T(2,128)S(1)} %copy.143), kind=kLoop, calls=%fused_computation.9 | loop fusion | flops 131072 | bytes 794624 | tf_op jit(solution)/shard_map/add | solution.py:97
  345.6 10.7 %all-to-all-start = ((f32[128,1,128]{2,1,0:T(1,128)}), f32[128,1,128]{2,1,0:T(1,128)}, u32[]{:S(2)}, u32[]{:S(2)}) async-start(f32[128,1,128]{2,1,0:T(1,128)} %reshape.174), calls=%async_computation | async-start | bytes 131072 | tf_op jit(solution)/shard_map/all_to_all | solution.py:55
  356.3 5.9 %fusion = f32[16,2,2,2048]{3,0,2,1:T(8,128)S(1)} fusion(bf16[2,2048,1024]{2,1,0:T(8,128)(2,1)} %param.15, bf16[16,2,1024,1]{2,0,1,3:T(8,128)(2,1)S(1)} %reshape.166), kind=kOutput, calls=%fused_computation.5 | convolution fusion | flops 268435456 | bytes 8978432 | tf_op jit(solution)/shard_map/dot_general | solution.py:104
  363.2 2.5 all-to-all-done
  365.8 4.4 all-to-all-start.2
  373.9 16.9 %scatter_fusion = f32[16,2,2048]{0,1,2:T(2,128)S(1)} fusion(f32[16,2,2048]{0,1,2:T(2,128)S(1)} %copy-done, s32[256]{0:T(256)S(1)} %get-tuple-element.25, f32[256,16,2]{1,2,0:T(2,128)} %get-tuple-element.32), kind=kCustom, calls=%fused_computation.3 | custom fusion | flops 8192 | bytes 99328 | tf_op jit(solution)/shard_map/scatter-add | solution.py:147
  397.8 8.5 %psum.84 = f32[32,16]{0,1:T(8,128)S(1)} all-reduce(f32[32,16]{0,1:T(8,128)S(1)} %fusion.3), channel_id=1, replica_groups=mesh['row_0'=4,'row_1'=2,'col_0'=4,'col_1'=4] {'row_0'}, use_global_device_ids=true, to_apply=%region_3.4 | all-reduce | flops 512 | bytes 4096 | tf_op jit(solution)/shard_map/psum | solution.py:60
  406.4 5.0 %psum.85 = f32[32,16]{0,1:T(8,128)S(1)} all-reduce(f32[32,16]{0,1:T(8,128)S(1)} %psum.84), channel_id=1, replica_groups=mesh['row_0'=4,'row_1'=2,'col_0'=4,'col_1'=4] {'row_1'}, use_global_device_ids=true, to_apply=%region_4.5 | all-reduce | flops 512 | bytes 4096 | tf_op jit(solution)/shard_map/psum | solution.py:60
  411.4 8.9 %psum.86 = f32[32,16]{0,1:T(8,128)S(1)} all-reduce(f32[32,16]{0,1:T(8,128)S(1)} %psum.85), channel_id=1, replica_groups=mesh['row_0'=4,'row_1'=2,'col_0'=4,'col_1'=4] {'col_0'}, use_global_device_ids=true, to_apply=%region_5.6 | all-reduce | flops 512 | bytes 4096 | tf_op jit(solution)/shard_map/psum | solution.py:60
  420.3 9.3 %psum.87 = f32[32,16]{0,1:T(8,128)S(1)} all-reduce(f32[32,16]{0,1:T(8,128)S(1)} %psum.86), channel_id=1, replica_groups=mesh['row_0'=4,'row_1'=2,'col_0'=4,'col_1'=4] {'col_1'}, use_global_device_ids=true, to_apply=%region_6.7 | all-reduce | flops 512 | bytes 4096 | tf_op jit(solution)/shard_map/psum | solution.py:60
  432.1 6.1 %psum.88 = f32[32,16]{0,1:T(8,128)S(1)} all-reduce(f32[32,16]{0,1:T(8,128)S(1)} %fusion.2), channel_id=1, replica_groups=mesh['row_0'=4,'row_1'=2,'col_0'=4,'col_1'=4] {'row_0'}, use_global_device_ids=true, to_apply=%region_7.8 | all-reduce | flops 512 | bytes 4096 | tf_op jit(solution)/shard_map/psum | solution.py:60
  438.2 8.3 %psum.89 = f32[32,16]{0,1:T(8,128)S(1)} all-reduce(f32[32,16]{0,1:T(8,128)S(1)} %psum.88), channel_id=1, replica_groups=mesh['row_0'=4,'row_1'=2,'col_0'=4,'col_1'=4] {'row_1'}, use_global_device_ids=true, to_apply=%region_8.9 | all-reduce | flops 512 | bytes 4096 | tf_op jit(solution)/shard_map/psum | solution.py:60
  446.5 6.1 %psum.90 = f32[32,16]{0,1:T(8,128)S(1)} all-reduce(f32[32,16]{0,1:T(8,128)S(1)} %psum.89), channel_id=1, replica_groups=mesh['row_0'=4,'row_1'=2,'col_0'=4,'col_1'=4] {'col_0'}, use_global_device_ids=true, to_apply=%region_9.10 | all-reduce | flops 512 | bytes 4096 | tf_op jit(solution)/shard_map/psum | solution.py:60
  452.6 6.1 %psum.91 = f32[32,16]{0,1:T(8,128)S(1)} all-reduce(f32[32,16]{0,1:T(8,128)S(1)} %psum.90), channel_id=1, replica_groups=mesh['row_0'=4,'row_1'=2,'col_0'=4,'col_1'=4] {'col_1'}, use_global_device_ids=true, to_apply=%region_10.11 | all-reduce | flops 512 | bytes 4096 | tf_op jit(solution)/shard_map/psum | solution.py:60
  460.2 7.8 %psum.92 = f32[16,16]{0,1:T(8,128)S(1)} all-reduce(f32[16,16]{0,1:T(8,128)S(1)} %fusion.4), channel_id=1, replica_groups=mesh['row_0'=4,'row_1'=2,'col_0'=4,'col_1'=4] {'row_0'}, use_global_device_ids=true, to_apply=%region_11.12 | all-reduce | flops 256 | bytes 2048 | tf_op jit(solution)/shard_map/psum | solution.py:60
  468.0 7.9 %psum.93 = f32[16,16]{0,1:T(8,128)S(1)} all-reduce(f32[16,16]{0,1:T(8,128)S(1)} %psum.92), channel_id=1, replica_groups=mesh['row_0'=4,'row_1'=2,'col_0'=4,'col_1'=4] {'row_1'}, use_global_device_ids=true, to_apply=%region_12.13 | all-reduce | flops 256 | bytes 2048 | tf_op jit(solution)/shard_map/psum | solution.py:60
  476.0 7.8 %psum.94 = f32[16,16]{0,1:T(8,128)S(1)} all-reduce(f32[16,16]{0,1:T(8,128)S(1)} %psum.93), channel_id=1, replica_groups=mesh['row_0'=4,'row_1'=2,'col_0'=4,'col_1'=4] {'col_0'}, use_global_device_ids=true, to_apply=%region_13.14 | all-reduce | flops 256 | bytes 2048 | tf_op jit(solution)/shard_map/psum | solution.py:60
  483.8 8.2 %psum.95 = f32[16,16]{0,1:T(8,128)S(1)} all-reduce(f32[16,16]{0,1:T(8,128)S(1)} %psum.94), channel_id=1, replica_groups=mesh['row_0'=4,'row_1'=2,'col_0'=4,'col_1'=4] {'col_1'}, use_global_device_ids=true, to_apply=%region_14.15 | all-reduce | flops 256 | bytes 2048 | tf_op jit(solution)/shard_map/psum | solution.py:60
  (98 shorter events, 43.1 us)
Async XLA Ops:
  0.6 20.0 %copy-start.3 = (f32[2,16,2,128]{3,2,1,0:T(2,128)S(1)}, f32[2,16,2,128]{3,2,1,0:T(2,128)}, u32[]{:S(2)}) copy-start(f32[2,16,2,128]{3,2,1,0:T(2,128)} %param.10) | copy-start | bytes 98308
  7.6 20.6 %copy-start.4 = (s32[16,2048]{1,0:T(8,128)S(1)}, s32[16,2048]{1,0:T(8,128)}, u32[]{:S(2)}) copy-start(s32[16,2048]{1,0:T(8,128)} %param.13) | copy-start | bytes 393220
  8.4 22.7 %collective-permute-start = (f32[16,2,128]{0,1,2:T(2,128)}, f32[16,2,128]{0,1,2:T(2,128)}, u32[]{:S(2)}, u32[]{:S(2)}) collective-permute-start(f32[16,2,128]{0,1,2:T(2,128)} %get-tuple-element.29), channel_id=1, source_target_pairs={{0,1},{1,2},{2,3},{3,4},{4,5},{5,6},{6,7},{7,8},{8,9},{9,10},{10,1... | collective-permute-start | bytes 49160 | tf_op jit(solution)/shard_map/ppermute | solution.py:20
  13.0 19.6 %collective-permute-start.1 = (f32[16,2,128]{0,1,2:T(2,128)}, f32[16,2,128]{0,1,2:T(2,128)}, u32[]{:S(2)}, u32[]{:S(2)}) collective-permute-start(f32[16,2,128]{0,1,2:T(2,128)} %get-tuple-element.28), channel_id=1, source_target_pairs={{1,0},{2,1},{3,2},{4,3},{5,4},{6,5},{7,6},{8,7},{9,8},{10,9},{11,1... | collective-permute-start | bytes 49160 | tf_op jit(solution)/shard_map/ppermute | solution.py:20
  14.3 19.9 %collective-permute-start.2 = (f32[16,2,128]{0,1,2:T(2,128)}, f32[16,2,128]{0,1,2:T(2,128)}, u32[]{:S(2)}, u32[]{:S(2)}) collective-permute-start(f32[16,2,128]{0,1,2:T(2,128)} %get-tuple-element.27), channel_id=1, source_target_pairs={{0,16},{16,32},{32,48},{48,64},{64,80},{80,96},{96,112},{1,17},{17... | collective-permute-start | bytes 49160 | tf_op jit(solution)/shard_map/ppermute | solution.py:20
  18.7 17.1 %collective-permute-start.3 = (f32[16,2,128]{0,1,2:T(2,128)}, f32[16,2,128]{0,1,2:T(2,128)}, u32[]{:S(2)}, u32[]{:S(2)}) collective-permute-start(f32[16,2,128]{0,1,2:T(2,128)} %get-tuple-element.26), channel_id=1, source_target_pairs={{16,0},{32,16},{48,32},{64,48},{80,64},{96,80},{112,96},{17,1},{33... | collective-permute-start | bytes 49160 | tf_op jit(solution)/shard_map/ppermute | solution.py:20
  21.3 324.3 %all-to-all-start.1 = ((bf16[8,16,2,128]{3,1,2,0:T(8,128)(2,1)}), bf16[8,16,2,128]{3,1,2,0:T(8,128)(2,1)S(1)}, u32[]{:S(2)}, u32[]{:S(2)}) async-start(bf16[8,16,2,128]{3,1,2,0:T(8,128)(2,1)} %broadcast_in_dim.65), calls=%async_computation.1 | async-start | bytes 131072 | tf_op jit(solution)/shard_map/all_to_all | solution.py:25
  26.8 2.6 copy-start.7
  26.8 4.0 copy-start.1
  37.3 224.2 %copy-start.5 = (f32[16,2048]{1,0:T(8,128)S(1)}, f32[16,2048]{1,0:T(8,128)}, u32[]{:S(2)}) copy-start(f32[16,2048]{1,0:T(8,128)} %param.12) | copy-start | bytes 393220
  261.6 77.4 %copy-start.6 = (f32[2048]{0:T(1024)S(1)}, f32[2048]{0:T(1024)}, u32[]{:S(2)}) copy-start(f32[2048]{0:T(1024)} %param.11) | copy-start | bytes 24580
  345.6 20.2 %all-to-all-start = ((f32[128,1,128]{2,1,0:T(1,128)}), f32[128,1,128]{2,1,0:T(1,128)}, u32[]{:S(2)}, u32[]{:S(2)}) async-start(f32[128,1,128]{2,1,0:T(1,128)} %reshape.174), calls=%async_computation | async-start | bytes 131072 | tf_op jit(solution)/shard_map/all_to_all | solution.py:55
  362.3 11.7 %copy-start = (f32[16,2,2048]{0,1,2:T(2,128)S(1)}, f32[16,2,2048]{0,1,2:T(2,128)}, u32[]{:S(2)}) copy-start(f32[16,2,2048]{0,1,2:T(2,128)} %bitcast_add_fusion) | copy-start | bytes 786436
  365.8 30.5 %all-to-all-start.2 = ((f32[16,16,2,128]{3,1,2,0:T(8,128)}), f32[16,16,2,128]{3,1,2,0:T(8,128)}, u32[]{:S(2)}, u32[]{:S(2)}) async-start(f32[16,16,2,128]{3,1,2,0:T(8,128)} %maximum_bitcast_fusion), calls=%async_computation.2 | async-start | bytes 524288 | tf_op jit(solution)/shard_map/all_to_all | solution.py:48
  390.8 6.5 %copy-start.2 = (f32[16,2,256]{0,1,2:T(2,128)S(1)}, f32[16,2,256]{0,1,2:T(2,128)}, u32[]{:S(2)}) copy-start(f32[16,2,256]{0,1,2:T(2,128)} %get-tuple-element.33) | copy-start | bytes 98308
  390.8 6.5 %copy-start.8 = (s32[128]{0:T(128)S(1)}, s32[128]{0:T(128)}, u32[]{:S(2)}) copy-start(s32[128]{0:T(128)} %param.17) | copy-start | bytes 1540
where the time goes:
time: 505 us; the launch traced here: 500 us
  local copies, waits for them, and re-layouts  249 us (49%)
  other arithmetic  113 us (22%)
  blocking collectives  90.2 us (18%)
  starting transfers between devices  32.7 us (6%)
  matrix products  11.7 us (2%)
    gather x1, local copies, waits for them, and re-layouts, fem_product(): gathered = jnp.take(extended, fem_columns, axis=2)  224 us
    psum x12, blocking collectives, one_axis_at_a_time(): return functools.reduce(lax.psum, axes, shard)  90.2 us
    reduce_sum x1, other arithmetic, fem_product(): return fem_diagonal * vectors + jnp.sum(fem_values * gathered, axis=2)  77.4 us
    scatter-add x1, other arithmetic, body(): fem_image = fem_image.at[:, :, clipped].add(answers * mask_row)  16.9 us
    unnamed x35, local copies, waits for them, and re-layouts  12.7 us
    ppermute x4, starting transfers between devices, passed_along(): return lax.ppermute(shard, axis, pairs)  12.2 us
    all_to_all x1, starting transfers between devices, sent_together(): lax.all_to_all(both, axis, split_axis=split_dim, concat_axis=concat_dim,...  10.7 us
  transfers between devices with their start and end apart: 7, of which 1 were waited for; matrix products, arithmetic and copies ran while one was open for 70% of the time, Pallas kernels for 0%

commit v1 on v0

v1 whole, which is shorter than its diff:
```python
import functools

import jax
import jax.numpy as jnp
from jax import lax
from jax.experimental import pallas as pl
from jax.experimental.pallas import tpu as pltpu
from jax.sharding import PartitionSpec as P

F32 = jnp.float32
BF16 = jnp.bfloat16
MESH = pl.DeviceIdType.MESH
HIGHEST = lax.Precision.HIGHEST
ROWS, COLS = 8, 16
DEVICES = ROWS * COLS
VEC = 32
LOCAL = 2048
PIECE = 128
WIDE = LOCAL + PIECE
COUNT = 2.0 * DEVICES * (LOCAL + PIECE)
NT = (((1,), (1,)), ((), ()))


def split2(x):
    high = x.astype(BF16)
    return high, (x - high.astype(F32)).astype(BF16)


def split3(x):
    high = x.astype(BF16)
    rest = x - high.astype(F32)
    mid = rest.astype(BF16)
    return high, mid, (rest - mid.astype(F32)).astype(BF16)


def lane_gather(table, lanes):
    return jnp.take_along_axis(table, lanes, axis=1, mode="promise_in_bounds")


def small_dot(a, b, dims):
    return lax.dot_general(a, b, (dims, ((), ())), precision=HIGHEST, preferred_element_type=F32)


def kernel(
    fem, bem, diag, vals, cols, halo, mat, trace, slot,
    next_fem, next_bem, hess, rfac,
    pieces, halo_out, halo_in, phi, partial, arrived, swap_out, swap_in,
    mat_buf, image, zp, pack, sum_out, col_in, row_in,
    mat_sem, halo_send, halo_recv, phi_send, phi_recv, part_send, part_recv,
    swap_send, swap_recv, col_send, col_recv, row_send, row_recv,
):
    r = lax.axis_index("row")
    c = lax.axis_index("col")
    me = r * COLS + c

    def matrix_copy(k):
        chunk = lax.rem(k + c // 2, 8)
        rows = pl.ds(pl.multiple_of(chunk * 256, 256), 256)
        return pltpu.make_async_copy(mat.at[:, rows, :], mat_buf.at[:, rows, :], mat_sem.at[k])

    for k in range(8):
        matrix_copy(k).start()

    def remote(src, dst, send, recv, row, col):
        return pltpu.make_async_remote_copy(
            src_ref=src, dst_ref=dst, send_sem=send, recv_sem=recv,
            device_id={"row": row, "col": col}, device_id_type=MESH,
        )

    def wait_bytes(ref, sem):
        pltpu.make_async_copy(ref, ref, sem).wait()

    phi_mine = bem[1].astype(BF16)
    mine = pl.ds(pl.multiple_of(r * PIECE, PIECE), PIECE)
    phi[:, mine] = phi_mine

    def send_phi(k, _):
        other = lax.rem(r + k, ROWS)
        remote(phi.at[:, mine], phi.at[:, mine], phi_send, phi_recv, other, c).start()
        return 0

    lax.fori_loop(1, ROWS, send_phi, 0)

    def picked(rows):
        rows = jnp.broadcast_to(rows, (VEC, 128))
        high = rows >> 7
        low = rows & 127
        out = jnp.zeros((VEC, 128), F32)
        for t in range(LOCAL // 128):
            out = jnp.where(high == t, lane_gather(fem[1, :, t * 128 : (t + 1) * 128], low), out)
        return out

    lane = lax.broadcasted_iota(jnp.int32, (8, 128), 1)
    trace_lo = jnp.broadcast_to(trace[:, :128], (8, 128))
    trace_hi = jnp.broadcast_to(trace[:, 128:], (8, 128))
    trace_q = []
    for q in range(2):
        source = (2 * lane + q) & 127
        full = jnp.where(lane < 64, lane_gather(trace_lo, source), lane_gather(trace_hi, source))
        trace_q.append(full[:1])

    for d in range(4):
        halo_out[d] = picked(halo[d : d + 1, :])

    for d, missing in enumerate((c == 0, c == COLS - 1, r == 0, r == ROWS - 1)):

        @pl.when(missing)
        def _(d=d):
            halo_in[d] = jnp.zeros((VEC, 128), F32)

    @pl.when(c + 1 < COLS)
    def _():
        remote(halo_out.at[0], halo_in.at[0], halo_send.at[0], halo_recv.at[0], r, c + 1).start()

    @pl.when(c > 0)
    def _():
        remote(halo_out.at[1], halo_in.at[1], halo_send.at[1], halo_recv.at[1], r, c - 1).start()

    @pl.when(r + 1 < ROWS)
    def _():
        remote(halo_out.at[2], halo_in.at[2], halo_send.at[2], halo_recv.at[2], r + 1, c).start()

    @pl.when(r > 0)
    def _():
        remote(halo_out.at[3], halo_in.at[3], halo_send.at[3], halo_recv.at[3], r - 1, c).start()

    leaving = [picked(jnp.maximum(t, 0)) * (t >= 0).astype(F32) for t in trace_q]
    owner = lax.broadcasted_iota(jnp.int32, (2 * DEVICES, PIECE), 0)
    owner = jnp.where(owner < DEVICES, 2 * owner, 2 * (owner - DEVICES) + 1)
    places = (owner == slot[...]).astype(F32).astype(BF16)
    back = lax.dot_general(
        jnp.concatenate(split3(bem[1]), axis=0), places, NT, preferred_element_type=F32
    )
    back = back[:VEC] + back[VEC : 2 * VEC] + back[2 * VEC :]
    swap_out[...] = jnp.concatenate(leaving + [back[:, :128], back[:, 128:]], axis=0).T

    def send_swap(k, _):
        other = lax.rem(me + k, DEVICES)
        remote(
            swap_out.at[pl.ds(other, 1)], swap_in.at[pl.ds(me, 1)], swap_send, swap_recv,
            other // COLS, lax.rem(other, COLS),
        ).start()
        return 0

    lax.fori_loop(1, DEVICES, send_swap, 0)
    swap_in[pl.ds(me, 1)] = swap_out[pl.ds(me, 1)]

    for p in range(2):
        for b in range(2):
            rows = slice(b * 16, b * 16 + 16)
            part = slice(p * 16, p * 16 + 16)
            for a, x in enumerate(split3(fem[b, part, :])):
                zp[p, a * 48 + b * 16 : a * 48 + b * 16 + 16, :LOCAL] = x
            for a, x in enumerate(split3(bem[b, part, :])):
                zp[p, a * 48 + b * 16 : a * 48 + b * 16 + 16, LOCAL:] = x
    own = jnp.zeros((VEC, VEC), F32)
    for p in range(2):
        whole = jnp.concatenate([zp[p, a * 48 : a * 48 + 32, :] for a in range(3)], axis=0)
        for b in range(3):
            both = lax.dot_general(
                whole, zp[p, b * 48 : b * 48 + 32, :], NT, preferred_element_type=F32
            )
            own = own + both[:32] + both[32:64] + both[64:]
    pack[...] = jnp.zeros((48, 128), F32)
    pack[:32, :32] = own
    packed = pack[0:8, :]
    for g in range(1, 4):
        packed = packed + pltpu.roll(pack[8 * g : 8 * g + 8, :], 32 * g, 1)
    sum_out[0] = packed

    def reduce_cols(n):
        col_in[n, c] = sum_out[n]

        def send(k, _):
            other = lax.rem(c + k, COLS)
            remote(sum_out.at[n], col_in.at[n, c], col_send.at[n], col_recv.at[n], r, other).start()
            return 0

        lax.fori_loop(1, COLS, send, 0)

    def reduce_rows(n):
        wait_bytes(col_in.at[n, pl.ds(0, COLS - 1)], col_recv.at[n])
        total = col_in[n, 0]
        for k in range(1, COLS):
            total = total + col_in[n, k]
        row_in[n, r] = total

        def send(k, _):
            other = lax.rem(r + k, ROWS)
            remote(row_in.at[n, r], row_in.at[n, r], row_send.at[n], row_recv.at[n], other, c).start()
            return 0

        lax.fori_loop(1, ROWS, send, 0)

    def reduced(n):
        wait_bytes(row_in.at[n, pl.ds(0, ROWS - 1)], row_recv.at[n])
        total = row_in[n, 0]
        for k in range(1, ROWS):
            total = total + row_in[n, k]
        return total * (1.0 / COUNT)

    reduce_cols(0)

    wait_bytes(phi.at[:, pl.ds(0, (ROWS - 1) * PIECE)], phi_recv)
    phi_all = phi[...]
    turned = jnp.concatenate([-phi_all[16:], phi_all[:16]], axis=0)

    def multiply(k, _):
        chunk = lax.rem(k + c // 2, 8)
        matrix_copy(k).wait()
        rows = pl.ds(pl.multiple_of(chunk * 256, 256), 256)
        out = lax.dot_general(phi_all, mat_buf[0, rows, :], NT, preferred_element_type=F32)
        out = out + lax.dot_general(turned, mat_buf[1, rows, :], NT, preferred_element_type=F32)
        for half in range(2):
            other = 2 * chunk + half
            partial[other] = out[:, half * 128 : half * 128 + 128]

            @pl.when(other != c)
            def _():
                remote(partial.at[other], arrived.at[c], part_send, part_recv, r, other).start()

        return 0

    lax.fori_loop(0, 8, multiply, 0)
    arrived[c] = partial[c]
    reduce_rows(0)

    @pl.when(c > 0)
    def _():
        wait_bytes(halo_in.at[0], halo_recv.at[0])

    @pl.when(c + 1 < COLS)
    def _():
        wait_bytes(halo_in.at[1], halo_recv.at[1])

    @pl.when(r > 0)
    def _():
        wait_bytes(halo_in.at[2], halo_recv.at[2])

    @pl.when(r + 1 < ROWS)
    def _():
        wait_bytes(halo_in.at[3], halo_recv.at[3])

    for t in range(10):
        if t < 8:
            x = fem[1, :, t * 256 : (t + 1) * 256]
        else:
            x = jnp.concatenate([halo_in[2 * t - 16], halo_in[2 * t - 15]], axis=1)
        for a, piece in enumerate(split2(x)):
            pieces[a, t * 32 : t * 32 + 32, :] = piece

    def product(j, _):
        here = pl.ds(pl.multiple_of(j * 256, 256), 256)
        acc = diag[:, here] * fem[1, :, here]
        for k in range(16):
            column = cols[k : k + 1, here]
            low = column & 255
            high = column >> 8
            hot = (lax.broadcasted_iota(jnp.int32, (256, 256), 0) == low).astype(F32).astype(BF16)
            found = jnp.dot(pieces[0], hot, preferred_element_type=F32)
            found = found + jnp.dot(pieces[1], hot, preferred_element_type=F32)
            got = found[:32]
            for t in range(1, 10):
                got = jnp.where(
                    jnp.broadcast_to(high == t, (32, 256)), found[t * 32 : t * 32 + 32], got
                )
            acc = acc + vals[k : k + 1, here] * got
        image[:, here] = acc
        return 0

    lax.fori_loop(0, LOCAL // 256, product, 0)

    wait_bytes(swap_in.at[pl.ds(0, DEVICES - 1)], swap_recv)
    met = swap_in[...].T
    chosen = jnp.broadcast_to(slot[...], (VEC, PIECE))
    taken = jnp.where(
        (chosen & 1) == 0, lane_gather(met[:32], chosen >> 1), lane_gather(met[32:64], chosen >> 1)
    )
    answers = jnp.concatenate([met[64:96], met[96:]], axis=1)
    answers = jnp.concatenate(split3(answers), axis=0)
    targets = jnp.concatenate(trace_q, axis=1)
    for t in range(LOCAL // 256):
        row = lax.broadcasted_iota(jnp.int32, (256, 256), 0) + t * 256
        hot = (row == targets).astype(F32).astype(BF16)
        put = lax.dot_general(answers, hot, NT, preferred_element_type=F32)
        here = slice(t * 256, t * 256 + 256)
        image[:, here] = image[:, here] + put[:32] + put[32:64] + put[64:]
    wait_bytes(arrived.at[pl.ds(0, COLS - 1)], part_recv)
    bem_image = taken
    for k in range(COLS):
        bem_image = bem_image + arrived[k]
    for p in range(2):
        part = slice(p * 16, p * 16 + 16)
        for a, x in enumerate(split3(image[part, :])):
            zp[p, a * 48 + 32 : a * 48 + 48, :LOCAL] = x
        for a, x in enumerate(split3(bem_image[part, :])):
            zp[p, a * 48 + 32 : a * 48 + 48, LOCAL:] = x

    inner = jnp.zeros((48, 16), F32)
    for p in range(2):
        whole = zp[p]
        for b in range(3):
            both = lax.dot_general(
                whole, zp[p, b * 48 + 32 : b * 48 + 48, :], NT, preferred_element_type=F32
            )
            inner = inner + both[:48] + both[48:96] + both[96:]
    pack[...] = jnp.zeros((48, 128), F32)
    pack[:, :16] = inner
    packed = pack[0:8, :]
    for g in range(1, 6):
        packed = packed + pltpu.roll(pack[8 * g : 8 * g + 8, :], 16 * g, 1)
    sum_out[1] = packed
    reduce_cols(1)
    total = reduced(0)
    for g in range(4):
        pack[8 * g : 8 * g + 8, :] = total if g == 0 else pltpu.roll(total, 128 - 32 * g, 1)
    gram_q = pack[:32, :32]
    reduce_rows(1)
    total = reduced(1)
    for g in range(6):
        pack[8 * g : 8 * g + 8, :] = total if g == 0 else pltpu.roll(total, 128 - 16 * g, 1)
    one = pack[:32, :16]
    norm = pack[32:48, :16]

    both = 2.0 * one - small_dot(gram_q, one, ((1,), (0,)))
    hess[...] = both
    left = small_dot(gram_q, both, ((1,), (0,))) - one
    gram = norm + small_dot(both, left, ((0,), (0,))) - small_dot(one, both, ((0,), (0,)))
    row_id = lax.broadcasted_iota(jnp.int32, (16, 16), 0)
    col_id = lax.broadcasted_iota(jnp.int32, (16, 16), 1)
    work = (gram + gram.T) * 0.5
    inverse = (row_id == col_id).astype(F32)
    upper = jnp.zeros((16, 16), F32)
    lower_inv = jnp.zeros((16, 16), F32)
    for j in range(16):
        pivot = work[j : j + 1, j : j + 1]
        root = lax.rsqrt(pivot)
        root = root * (1.5 - 0.5 * pivot * root * root)
        line = jnp.broadcast_to(work[j : j + 1, :] * root, (16, 16))
        line_inv = jnp.broadcast_to(inverse[j : j + 1, :] * root, (16, 16))
        column = jnp.broadcast_to(work[:, j : j + 1] * root, (16, 16))
        upper = jnp.where((row_id == j) & (col_id >= j), line, upper)
        lower_inv = jnp.where(row_id == j, line_inv, lower_inv)
        work = work - column * line
        inverse = inverse - column * line_inv
    rfac[...] = upper

    weights = -small_dot(lower_inv, both, ((1,), (1,)))
    w_high, w_low = split2(weights)
    l_high, l_low = split2(lower_inv)
    w_pair = jnp.concatenate([w_high, w_low], axis=0)
    l_pair = jnp.concatenate([l_high, l_low], axis=0)
    for p in range(2):
        first = jnp.dot(w_pair, zp[p, 0:32, :], preferred_element_type=F32)
        first = first + jnp.dot(l_pair, zp[p, 32:48, :], preferred_element_type=F32)
        second = jnp.dot(w_high, zp[p, 48:80, :], preferred_element_type=F32)
        second = second + jnp.dot(l_high, zp[p, 80:96, :], preferred_element_type=F32)
        made = first[:16] + first[16:] + second
        next_fem[p] = made[:, :LOCAL]
        next_bem[p] = made[:, LOCAL:]

    @pl.when(c + 1 < COLS)
    def _():
        wait_bytes(halo_out.at[0], halo_send.at[0])

    @pl.when(c > 0)
    def _():
        wait_bytes(halo_out.at[1], halo_send.at[1])

    @pl.when(r + 1 < ROWS)
    def _():
        wait_bytes(halo_out.at[2], halo_send.at[2])

    @pl.when(r > 0)
    def _():
        wait_bytes(halo_out.at[3], halo_send.at[3])

    wait_bytes(phi.at[:, pl.ds(0, (ROWS - 1) * PIECE)], phi_send)
    wait_bytes(arrived.at[pl.ds(0, COLS - 1)], part_send)
    wait_bytes(swap_in.at[pl.ds(0, DEVICES - 1)], swap_send)
    for n in range(2):
        wait_bytes(col_in.at[n, pl.ds(0, COLS - 1)], col_send.at[n])
        wait_bytes(row_in.at[n, pl.ds(0, ROWS - 1)], row_send.at[n])


def body(fem_basis, bem_basis, diag, vals, cols, halo, mat, trace, slot):
    fem = jnp.transpose(fem_basis, (0, 2, 1, 3)).reshape(2, VEC, LOCAL)
    bem = jnp.transpose(bem_basis, (0, 2, 1, 3)).reshape(2, VEC, PIECE)
    vmem = pl.BlockSpec(memory_space=pltpu.VMEM)
    dma = pltpu.SemaphoreType.DMA
    next_fem, next_bem, hess, rfac = pl.pallas_call(
        kernel,
        out_shape=(
            jax.ShapeDtypeStruct((2, 16, LOCAL), F32),
            jax.ShapeDtypeStruct((2, 16, PIECE), F32),
            jax.ShapeDtypeStruct((VEC, 16), F32),
            jax.ShapeDtypeStruct((16, 16), F32),
        ),
        in_specs=[vmem] * 6 + [pl.BlockSpec(memory_space=pl.ANY)] + [vmem] * 2,
        out_specs=(vmem,) * 4,
        scratch_shapes=[
            pltpu.VMEM((2, 320, 256), BF16),
            pltpu.VMEM((4, VEC, 128), F32),
            pltpu.VMEM((4, VEC, 128), F32),
            pltpu.VMEM((VEC, ROWS * PIECE), BF16),
            pltpu.VMEM((COLS, VEC, PIECE), F32),
            pltpu.VMEM((COLS, VEC, PIECE), F32),
            pltpu.VMEM((DEVICES, 128), F32),
            pltpu.VMEM((DEVICES, 128), F32),
            pltpu.VMEM((2, 2048, 1024), BF16),
            pltpu.VMEM((VEC, LOCAL), F32),
            pltpu.VMEM((2, 144, WIDE), BF16),
            pltpu.VMEM((48, 128), F32),
            pltpu.VMEM((2, 8, 128), F32),
            pltpu.VMEM((2, COLS, 8, 128), F32),
            pltpu.VMEM((2, ROWS, 8, 128), F32),
            dma((8,)),
            dma((4,)),
            dma((4,)),
            dma, dma, dma, dma, dma, dma,
            dma((2,)), dma((2,)), dma((2,)), dma((2,)),
        ],
        compiler_params=pltpu.CompilerParams(
            has_side_effects=True, vmem_limit_bytes=40 << 20
        ),
    )(fem, bem, diag.reshape(1, LOCAL), vals, cols, halo, mat, trace.reshape(1, 256), slot.reshape(1, PIECE))
    return (
        jnp.transpose(next_fem, (1, 0, 2)),
        jnp.transpose(next_bem, (1, 0, 2)),
        hess.reshape(2, 16, 16),
        rfac,
    )


def solution(mesh):
    both = ("row", "col")
    return jax.shard_map(
        body,
        mesh=mesh,
        in_specs=(
            P(None, None, None, both), P(None, None, None, both), P(both), P(None, both),
            P(None, both), P(None, both), P(None, "row", "col"), P(both), P(both),
        ),
        out_specs=(P(None, None, both), P(None, None, both), P(), P()),
        check_vma=False,
    )
```

time: 505 us -> 66.8 us (0.13)
  local copies, waits for them, and re-layouts: 249 us -> 12.7 us
  other arithmetic: 113 us -> 0 us
  blocking collectives: 90.2 us -> 0 us
  Pallas kernels: 0 us -> 53 us
  starting transfers between devices: 32.7 us -> 0 us
  matrix products: 11.7 us -> 0 us
    gather x4 -> x0, local copies, waits for them, and re-layouts: 227 us -> none  [the longest x1 224 us: fem_product(): gathered = jnp.take(extended, fem_columns, axis=2)]
    psum x12 -> x0, blocking collectives: 90.2 us -> none  [one_axis_at_a_time(): return functools.reduce(lax.psum, axes, shard)]
    reduce_sum x2 -> x0, other arithmetic: 78.4 us -> none  [the longest x1 77.4 us: fem_product(): return fem_diagonal * vectors + jnp.sum(fem_values * gathered, axis=2)]
    pallas_call x0 -> x1, Pallas kernels: none -> 53 us  [body(): pl.pallas_call(kernel, out_shape=(jax.ShapeDtypeStruct((2, 16, LOCAL), F3...]
    all_to_all x3 -> x0, starting transfers between devices: 20.6 us -> none  [the longest x1 10.7 us: sent_together(): lax.all_to_all(both, axis, split_axis=split_dim, concat_axis=concat_dim,...]
    scatter-add x1 -> x0, other arithmetic: 16.9 us -> none  [body(): fem_image = fem_image.at[:, :, clipped].add(answers * mask_row)]
    ppermute x4 -> x0, starting transfers between devices: 12.2 us -> none  [passed_along(): return lax.ppermute(shard, axis, pairs)]
    dot_general x15 -> x0, matrix products: 11.5 us -> none  [the longest x1 5.93 us: bem_product(): lax.dot_general(flat_part, bem_matrix, (((1,), (2,)), ((), ())), preferre...]
  transfers between devices with their start and end apart: 7 -> 0, of which waited for: 1 -> 0; matrix products, arithmetic and copies ran while one was open for 70% -> 0% of each run, Pallas kernels for 0% -> 0%
where the time goes in v1:
time: 66.8 us; the launch traced here: 66.4 us
  Pallas kernels  53 us (79%)
  local copies, waits for them, and re-layouts  12.7 us (19%)
    pallas_call x1, Pallas kernels, body(): pl.pallas_call(kernel, out_shape=(jax.ShapeDtypeStruct((2, 16, LOCAL), F3...  53 us
    unnamed x18, local copies, waits for them, and re-layouts  10.6 us
    transpose x1, local copies, waits for them, and re-layouts, body(): fem = jnp.transpose(fem_basis, (0, 2, 1, 3)).reshape(2, VEC, LOCAL)  1.35 us

profile of v1, /device:TPU:1, one launch (start us, length us, event | category | flops | bytes accessed | tf_op | source)
XLA Modules:
  0.0 66.4 jit_solution(9871524165920648877)
XLA Ops:
  0.6 0.8 %copy.14 = f32[2,2,16,128]{3,2,1,0:T(8,128)S(1)} copy(f32[2,2,16,128]{3,1,2,0:T(2,128)} %bitcast.19) | data formatting | bytes 65536 | tf_op jit(solution)/shard_map/transpose | solution.py:388
  1.4 1.3 %copy.13 = f32[2,2,16,2048]{3,2,1,0:T(8,128)S(1)} copy(f32[2,2,16,2048]{3,1,2,0:T(2,128)} %bitcast.18) | data formatting | bytes 1048576 | tf_op jit(solution)/shard_map/transpose | solution.py:387
  2.7 0.0 copy-start
  2.8 3.4 %copy-done = bf16[2,2048,1024]{2,1,0:T(8,128)(2,1)S(1)} copy-done((bf16[2,2048,1024]{2,1,0:T(8,128)(2,1)S(1)}, bf16[2,2048,1024]{2,1,0:T(8,128)(2,1)}, u32[]{:S(2)}) %copy-start) | copy-done | bytes 8388632
  6.1 0.0 copy-start.1
  6.1 0.9 %copy-done.1 = f32[16,2048]{1,0:T(8,128)S(1)} copy-done((f32[16,2048]{1,0:T(8,128)S(1)}, f32[16,2048]{1,0:T(8,128)}, u32[]{:S(2)}) %copy-start.1) | copy-done | bytes 131096
  7.0 0.0 copy-start.2
  7.0 0.9 %copy-done.2 = s32[16,2048]{1,0:T(8,128)S(1)} copy-done((s32[16,2048]{1,0:T(8,128)S(1)}, s32[16,2048]{1,0:T(8,128)}, u32[]{:S(2)}) %copy-start.2) | copy-done | bytes 131096
  7.9 0.0 copy-start.3
  7.9 0.7 %copy-done.3 = f32[2048]{0:T(1024)S(1)} copy-done((f32[2048]{0:T(1024)S(1)}, f32[2048]{0:T(1024)}, u32[]{:S(2)}) %copy-start.3) | copy-done | bytes 8216
  8.6 0.0 copy-start.4
  8.6 0.7 %copy-done.4 = s32[4,128]{1,0:T(4,128)S(1)} copy-done((s32[4,128]{1,0:T(4,128)S(1)}, s32[4,128]{1,0:T(4,128)}, u32[]{:S(2)}) %copy-start.4) | copy-done | bytes 2072
  9.3 0.0 copy-start.5
  9.3 0.7 %copy-done.5 = s32[256]{0:T(256)S(1)} copy-done((s32[256]{0:T(256)S(1)}, s32[256]{0:T(256)}, u32[]{:S(2)}) %copy-start.5) | copy-done | bytes 1048
  10.0 0.0 copy-start.6
  10.0 0.7 copy-done.6
  10.7 53.0 %shard_map.120 = (f32[2,16,2048]{2,1,0:T(8,128)S(1)}, f32[2,16,128]{2,1,0:T(8,128)S(1)}, f32[32,16]{1,0:T(8,128)S(1)}, f32[16,16]{1,0:T(8,128)S(1)}) custom-call(f32[2,32,2048]{2,1,0:T(8,128)S(1)} %bitcast.10, f32[2,32,128]{2,1,0:T(8,128)S(1)} %bitcast.12, f32[1,2048]{1,0:T(1,128)S(1)} %bitcast.15, f32[16,2048]{1,0:T(8,128)S(1)} %copy-done.1, ...), custom_call_target="tpu_custom_call" | custom-call | tf_op jit(solution)/shard_map/pallas_call | solution.py:391
  63.7 0.9 %copy.15 = f32[16,2,2048]{2,1,0:T(2,128)} copy(f32[16,2,2048]{2,0,1:T(8,128)S(1)} %bitcast.11) | data formatting | bytes 524288
  64.6 0.6 copy.16
  65.2 0.6 copy.19
  65.8 0.6 copy.20
Async XLA Ops:
  2.7 3.4 %copy-start = (bf16[2,2048,1024]{2,1,0:T(8,128)(2,1)S(1)}, bf16[2,2048,1024]{2,1,0:T(8,128)(2,1)}, u32[]{:S(2)}) copy-start(bf16[2,2048,1024]{2,1,0:T(8,128)(2,1)} %mat.1) | copy-start | bytes 25165828
  6.1 0.9 %copy-start.1 = (f32[16,2048]{1,0:T(8,128)S(1)}, f32[16,2048]{1,0:T(8,128)}, u32[]{:S(2)}) copy-start(f32[16,2048]{1,0:T(8,128)} %vals.1) | copy-start | bytes 393220
  7.0 0.9 %copy-start.2 = (s32[16,2048]{1,0:T(8,128)S(1)}, s32[16,2048]{1,0:T(8,128)}, u32[]{:S(2)}) copy-start(s32[16,2048]{1,0:T(8,128)} %cols.1) | copy-start | bytes 393220
  7.9 0.7 %copy-start.3 = (f32[2048]{0:T(1024)S(1)}, f32[2048]{0:T(1024)}, u32[]{:S(2)}) copy-start(f32[2048]{0:T(1024)} %param.11) | copy-start | bytes 24580
  8.6 0.7 %copy-start.4 = (s32[4,128]{1,0:T(4,128)S(1)}, s32[4,128]{1,0:T(4,128)}, u32[]{:S(2)}) copy-start(s32[4,128]{1,0:T(4,128)} %halo.1) | copy-start | bytes 6148
  9.3 0.7 %copy-start.5 = (s32[256]{0:T(256)S(1)}, s32[256]{0:T(256)}, u32[]{:S(2)}) copy-start(s32[256]{0:T(256)} %param.16) | copy-start | bytes 3076
  10.0 0.7 copy-start.6

commit v2 on v1

v2 whole, which is shorter than its diff:
```python
import functools

import jax
import jax.numpy as jnp
from jax import lax
from jax.experimental import pallas as pl
from jax.experimental.pallas import tpu as pltpu
from jax.sharding import PartitionSpec as P

F32 = jnp.float32
BF16 = jnp.bfloat16
MESH = pl.DeviceIdType.MESH
HIGHEST = lax.Precision.HIGHEST
ROWS, COLS = 8, 16
DEVICES = ROWS * COLS
VEC = 32
LOCAL = 2048
PIECE = 128
WIDE = LOCAL + PIECE
COUNT = 2.0 * DEVICES * (LOCAL + PIECE)
NT = (((1,), (1,)), ((), ()))
BY_LANE_NEAR = (1, 4, 7, 10, 13)
BY_LANE_FAR = (1, 3, 5, 7, 9, 11, 13)
FIRST_CHUNKS = 4


def split2(x):
    high = x.astype(BF16)
    return high, (x - high.astype(F32)).astype(BF16)


def split3(x):
    high = x.astype(BF16)
    rest = x - high.astype(F32)
    mid = rest.astype(BF16)
    return high, mid, (rest - mid.astype(F32)).astype(BF16)


def lane_gather(table, lanes):
    return jnp.take_along_axis(table, lanes, axis=1, mode="promise_in_bounds")


def small_dot(a, b, dims):
    return lax.dot_general(a, b, (dims, ((), ())), precision=HIGHEST, preferred_element_type=F32)


def looked_up(table, column, tiles, first):
    halves = []
    for half in range(2):
        here = jnp.broadcast_to(column[:, half * 128 : half * 128 + 128], (VEC, 128))
        low = here & 127
        high = here >> 7
        got = jnp.zeros((VEC, 128), F32)
        for t in range(tiles):
            got = jnp.where(high == t + first, lane_gather(table(t), low), got)
        halves.append(got)
    return jnp.concatenate(halves, axis=1)


def multiplied_up(pieces, column, tiles, first):
    low = jnp.broadcast_to((column & 255).astype(jnp.int16), (256, 256))
    high = column >> 8
    hot = jnp.where(
        lax.broadcasted_iota(jnp.int16, (256, 256), 0) == low,
        jnp.ones((256, 256), BF16),
        jnp.zeros((256, 256), BF16),
    )
    found = jnp.dot(pieces, hot, preferred_element_type=F32)
    found = found[: tiles * VEC] + found[tiles * VEC :]
    got = jnp.zeros((VEC, 256), F32)
    for t in range(tiles):
        here = jnp.broadcast_to(high == t + first, (VEC, 256))
        got = jnp.where(here, found[t * VEC : t * VEC + VEC], got)
    return got


def step_kernel(
    fem_hbm, bem_hbm, diag_hbm, vals_hbm, cols_hbm, halo_hbm, mat, trace_hbm, slot_hbm,
    w_hbm, sums,
    fem, bem, diag, vals, cols, halo, trace, slot, in_sem, out_sem,
    near, far, halo_out, halo_in, phi, partial, arrived, swap_out, swap_mid, swap_in,
    mat_buf, image, zp, pack, sum_out, col_in, row_in,
    mat_sem, halo_send, halo_recv, phi_send, phi_recv, part_send, part_recv,
    mid_send, mid_recv, swap_send, swap_recv, col_send, col_recv, row_send, row_recv,
):
    r = lax.axis_index("row")
    c = lax.axis_index("col")

    barrier = pltpu.get_barrier_semaphore()

    def greet_col(k, _):
        there = {"row": r, "col": lax.rem(c + k, COLS)}
        pl.semaphore_signal(barrier, inc=1, device_id=there, device_id_type=MESH)
        return 0

    def greet_row(k, _):
        there = {"row": lax.rem(r + k, ROWS), "col": c}
        pl.semaphore_signal(barrier, inc=1, device_id=there, device_id_type=MESH)
        return 0

    lax.fori_loop(1, ROWS, greet_row, 0)
    lax.fori_loop(1, COLS, greet_col, 0)

    loads = {}

    def load(name, pairs):
        first = 4 * len(loads)
        loads[name] = [
            pltpu.make_async_copy(a, b, in_sem.at[first + i]) for i, (a, b) in enumerate(pairs)
        ]
        for copy in loads[name]:
            copy.start()

    def ready(*names):
        for name in names:
            for copy in loads[name]:
                copy.wait()

    def parts(whole, held, blocks):
        return [
            (whole.at[b, :, p, :], held.at[b, pl.ds(p * 16, 16), :])
            for b in blocks
            for p in range(2)
        ]

    load("bem", parts(bem_hbm, bem, (0, 1)))
    load("fem", parts(fem_hbm, fem, (1,)))
    load("index", [(halo_hbm, halo), (trace_hbm, trace), (slot_hbm, slot)])
    load("sparse", [(cols_hbm, cols), (vals_hbm, vals), (diag_hbm, diag)])
    load("old", parts(fem_hbm, fem, (0,)))

    def matrix_copy(k):
        chunk = lax.rem(k + c // 2, 8)
        rows = pl.ds(pl.multiple_of(chunk * 256, 256), 256)
        return pltpu.make_async_copy(mat.at[:, rows, :], mat_buf.at[:, rows, :], mat_sem.at[k])

    for k in range(8):
        matrix_copy(k).start()

    def remote(src, dst, send, recv, row, col):
        return pltpu.make_async_remote_copy(
            src_ref=src, dst_ref=dst, send_sem=send, recv_sem=recv,
            device_id={"row": row, "col": col}, device_id_type=MESH,
        )

    def wait_bytes(ref, sem):
        pltpu.make_async_copy(ref, ref, sem).wait()

    ready("bem")
    mine = pl.ds(pl.multiple_of(r * PIECE, PIECE), PIECE)
    phi[:, mine] = bem[1].astype(BF16)

    ready("index", "fem")

    def picked(rows):
        rows = jnp.broadcast_to(rows, (VEC, 128))
        high = rows >> 7
        low = rows & 127
        out = jnp.zeros((VEC, 128), F32)
        for t in range(LOCAL // 128):
            out = jnp.where(high == t, lane_gather(fem[1, :, t * 128 : (t + 1) * 128], low), out)
        return out

    for d in range(4):
        halo_out[d] = picked(halo[d : d + 1, :])
    for d, missing in enumerate((c == 0, c == COLS - 1, r == 0, r == ROWS - 1)):

        @pl.when(missing)
        def _(d=d):
            halo_in[d] = jnp.zeros((VEC, 128), F32)

    lane = lax.broadcasted_iota(jnp.int32, (8, 128), 1)
    trace_lo = jnp.broadcast_to(trace[:, :128], (8, 128))
    trace_hi = jnp.broadcast_to(trace[:, 128:], (8, 128))
    trace_q = []
    for q in range(2):
        source = (2 * lane + q) & 127
        full = jnp.where(lane < 64, lane_gather(trace_lo, source), lane_gather(trace_hi, source))
        trace_q.append(full[:1])
    leaving = [picked(jnp.maximum(t, 0)) * (t >= 0).astype(F32) for t in trace_q]
    owner = lax.broadcasted_iota(jnp.int32, (2 * DEVICES, PIECE), 0)
    owner = jnp.where(owner < DEVICES, 2 * owner, 2 * (owner - DEVICES) + 1)
    places = (owner == slot[...]).astype(F32).astype(BF16)
    back = lax.dot_general(
        jnp.concatenate(split3(bem[1]), axis=0), places, NT, preferred_element_type=F32
    )
    back = back[:VEC] + back[VEC : 2 * VEC] + back[2 * VEC :]
    swap_out[...] = jnp.concatenate(leaving + [back[:, :128], back[:, 128:]], axis=0).T

    for t in range(8):
        for a, piece in enumerate(split2(fem[1, :, t * 256 : (t + 1) * 256])):
            near[a * 256 + t * 32 : a * 256 + t * 32 + 32, :] = piece
    ready("sparse")

    def product_near(j, _):
        here = pl.ds(pl.multiple_of(j * 256, 256), 256)
        acc = diag[:, here] * fem[1, :, here]
        for k in range(16):
            column = cols[k : k + 1, here]
            if k in BY_LANE_NEAR:
                got = looked_up(lambda t: fem[1, :, t * 128 : (t + 1) * 128], column, 16, 0)
            else:
                got = multiplied_up(near[...], column, 8, 0)
            acc = acc + vals[k : k + 1, here] * got
        image[:, here] = acc
        return 0

    lax.fori_loop(0, FIRST_CHUNKS, product_near, 0)

    pl.semaphore_wait(barrier, ROWS + COLS - 2)

    def send_phi(k, _):
        other = lax.rem(r + k, ROWS)
        remote(phi.at[:, mine], phi.at[:, mine], phi_send, phi_recv, other, c).start()
        return 0

    lax.fori_loop(1, ROWS, send_phi, 0)

    neighbours = (
        (c + 1 < COLS, r, c + 1, c > 0),
        (c > 0, r, c - 1, c + 1 < COLS),
        (r + 1 < ROWS, r + 1, c, r > 0),
        (r > 0, r - 1, c, r + 1 < ROWS),
    )
    for d, (exists, row, col, _) in enumerate(neighbours):

        @pl.when(exists)
        def _(d=d, row=row, col=col):
            remote(
                halo_out.at[d], halo_in.at[d], halo_send.at[d], halo_recv.at[d], row, col
            ).start()

    def send_mid(k, _):
        other = lax.rem(r + k, ROWS)
        block = pl.ds(pl.multiple_of(other * COLS, COLS), COLS)
        remote(swap_out.at[block], swap_mid.at[r], mid_send, mid_recv, other, c).start()
        return 0

    lax.fori_loop(1, ROWS, send_mid, 0)
    swap_mid[r] = swap_out[pl.ds(pl.multiple_of(r * COLS, COLS), COLS)]

    lax.fori_loop(FIRST_CHUNKS, LOCAL // 256, product_near, 0)

    wait_bytes(phi.at[:, pl.ds(0, (ROWS - 1) * PIECE)], phi_recv)
    phi_all = phi[...]
    turned = jnp.concatenate([-phi_all[16:], phi_all[:16]], axis=0)

    def multiply(k, _):
        chunk = lax.rem(k + c // 2, 8)
        matrix_copy(k).wait()
        rows = pl.ds(pl.multiple_of(chunk * 256, 256), 256)
        out = lax.dot_general(phi_all, mat_buf[0, rows, :], NT, preferred_element_type=F32)
        out = out + lax.dot_general(turned, mat_buf[1, rows, :], NT, preferred_element_type=F32)
        for half in range(2):
            other = 2 * chunk + half
            partial[other] = out[:, half * 128 : half * 128 + 128]

            @pl.when(other != c)
            def _():
                remote(partial.at[other], arrived.at[c], part_send, part_recv, r, other).start()

        return 0

    lax.fori_loop(0, 8, multiply, 0)
    arrived[c] = partial[c]

    wait_bytes(swap_mid.at[pl.ds(0, ROWS - 1)], mid_recv)

    def send_swap(k, _):
        other = lax.rem(c + k, COLS)
        remote(
            swap_mid.at[:, pl.ds(other, 1), :], swap_in.at[:, pl.ds(c, 1), :],
            swap_send, swap_recv, r, other,
        ).start()
        return 0

    lax.fori_loop(1, COLS, send_swap, 0)
    swap_in[:, pl.ds(c, 1), :] = swap_mid[:, pl.ds(c, 1), :]

    ready("old")
    for p in range(2):
        for b in range(2):
            rows = slice(p * 16, p * 16 + 16)
            for a, x in enumerate(split3(fem[b, rows, :])):
                zp[p, a * 48 + b * 16 : a * 48 + b * 16 + 16, :LOCAL] = x
            for a, x in enumerate(split3(bem[b, rows, :])):
                zp[p, a * 48 + b * 16 : a * 48 + b * 16 + 16, LOCAL:] = x
    own = jnp.zeros((VEC, VEC), F32)
    for p in range(2):
        whole = jnp.concatenate([zp[p, a * 48 : a * 48 + 32, :] for a in range(3)], axis=0)
        for b in range(3):
            both = lax.dot_general(
                whole, zp[p, b * 48 : b * 48 + 32, :], NT, preferred_element_type=F32
            )
            own = own + both[:32] + both[32:64] + both[64:]
    pack[...] = jnp.zeros((48, 128), F32)
    pack[:32, :32] = own
    packed = pack[0:8, :]
    for g in range(1, 4):
        packed = packed + pltpu.roll(pack[8 * g : 8 * g + 8, :], 32 * g, 1)
    sum_out[0] = packed

    def reduce_cols(n):
        col_in[n, c] = sum_out[n]

        def send(k, _):
            other = lax.rem(c + k, COLS)
            remote(sum_out.at[n], col_in.at[n, c], col_send.at[n], col_recv.at[n], r, other).start()
            return 0

        lax.fori_loop(1, COLS, send, 0)

    def reduce_rows(n):
        wait_bytes(col_in.at[n, pl.ds(0, COLS - 1)], col_recv.at[n])
        total = col_in[n, 0]
        for k in range(1, COLS):
            total = total + col_in[n, k]
        row_in[n, r] = total

        def send(k, _):
            other = lax.rem(r + k, ROWS)
            remote(row_in.at[n, r], row_in.at[n, r], row_send.at[n], row_recv.at[n], other, c).start()
            return 0

        lax.fori_loop(1, ROWS, send, 0)

    def reduced(n):
        wait_bytes(row_in.at[n, pl.ds(0, ROWS - 1)], row_recv.at[n])
        total = row_in[n, 0]
        for k in range(1, ROWS):
            total = total + row_in[n, k]
        return total * (1.0 / COUNT)

    reduce_cols(0)

    for d, (_, _, _, comes) in enumerate(neighbours):

        @pl.when(comes)
        def _(d=d):
            wait_bytes(halo_in.at[d], halo_recv.at[d])

    for t in range(2):
        x = jnp.concatenate([halo_in[2 * t], halo_in[2 * t + 1]], axis=1)
        for a, piece in enumerate(split2(x)):
            far[a * 64 + t * 32 : a * 64 + t * 32 + 32, :] = piece

    def product_far(j, _):
        here = pl.ds(pl.multiple_of(j * 256, 256), 256)
        acc = image[:, here]
        for k in range(16):
            column = cols[k : k + 1, here]
            if k in BY_LANE_FAR:
                got = looked_up(lambda t: halo_in[t], column, 4, 16)
            else:
                got = multiplied_up(far[...], column, 2, 8)
            acc = acc + vals[k : k + 1, here] * got
        image[:, here] = acc
        return 0

    lax.fori_loop(0, LOCAL // 256, product_far, 0)
    reduce_rows(0)

    wait_bytes(swap_in.at[:, pl.ds(0, COLS - 1), :], swap_recv)
    met = swap_in[...].reshape(DEVICES, 128).T
    chosen = jnp.broadcast_to(slot[...], (VEC, PIECE))
    taken = jnp.where(
        (chosen & 1) == 0, lane_gather(met[:32], chosen >> 1), lane_gather(met[32:64], chosen >> 1)
    )
    answers = jnp.concatenate([met[64:96], met[96:]], axis=1)
    answers = jnp.concatenate(split3(answers), axis=0)
    targets = jnp.concatenate(trace_q, axis=1)
    for t in range(LOCAL // 256):
        row = lax.broadcasted_iota(jnp.int32, (256, 256), 0) + t * 256
        hot = (row == targets).astype(F32).astype(BF16)
        put = lax.dot_general(answers, hot, NT, preferred_element_type=F32)
        here = slice(t * 256, t * 256 + 256)
        image[:, here] = image[:, here] + put[:32] + put[32:64] + put[64:]
    for p in range(2):
        for a, x in enumerate(split3(image[p * 16 : p * 16 + 16, :LOCAL])):
            zp[p, a * 48 + 32 : a * 48 + 48, :LOCAL] = x

    def inner(columns):
        made = jnp.zeros((48, 16), F32)
        for p in range(2):
            whole = zp[p, :, columns]
            for b in range(3):
                both = lax.dot_general(
                    whole, zp[p, b * 48 + 32 : b * 48 + 48, columns], NT,
                    preferred_element_type=F32,
                )
                made = made + both[:48] + both[48:96] + both[96:]
        return made

    pack[...] = jnp.zeros((48, 128), F32)
    pack[:, :16] = inner(slice(0, LOCAL))
    wait_bytes(arrived.at[pl.ds(0, COLS - 1)], part_recv)
    bem_image = taken
    for k in range(COLS):
        bem_image = bem_image + arrived[k]
    image[:, LOCAL:] = bem_image
    for p in range(2):
        for a, x in enumerate(split3(bem_image[p * 16 : p * 16 + 16, :])):
            zp[p, a * 48 + 32 : a * 48 + 48, LOCAL:] = x
    pack[:, :16] = pack[:, :16] + inner(slice(LOCAL, WIDE))
    packed = pack[0:8, :]
    for g in range(1, 6):
        packed = packed + pltpu.roll(pack[8 * g : 8 * g + 8, :], 16 * g, 1)
    sum_out[1] = packed
    reduce_cols(1)
    leave = pltpu.make_async_copy(image, w_hbm, out_sem)
    leave.start()
    sums[:8, :] = reduced(0)

    for d, (exists, _, _, _) in enumerate(neighbours):

        @pl.when(exists)
        def _(d=d):
            wait_bytes(halo_out.at[d], halo_send.at[d])

    wait_bytes(phi.at[:, pl.ds(0, (ROWS - 1) * PIECE)], phi_send)
    wait_bytes(arrived.at[pl.ds(0, COLS - 1)], part_send)
    wait_bytes(swap_mid.at[pl.ds(0, ROWS - 1)], mid_send)
    wait_bytes(swap_in.at[:, pl.ds(0, COLS - 1), :], swap_send)
    wait_bytes(col_in.at[0, pl.ds(0, COLS - 1)], col_send.at[0])
    wait_bytes(row_in.at[0, pl.ds(0, ROWS - 1)], row_send.at[0])
    reduce_rows(1)
    wait_bytes(col_in.at[1, pl.ds(0, COLS - 1)], col_send.at[1])
    leave.wait()
    sums[8:, :] = reduced(1)
    wait_bytes(row_in.at[1, pl.ds(0, ROWS - 1)], row_send.at[1])


def finish_kernel(
    fem_hbm, bem_hbm, w_hbm, sums, next_fem, next_bem, hess, rfac,
    basis, image, pack_q, pack, fem_out, bem_out, in_sem, out_sem,
):
    copies = []
    for b in range(2):
        for p in range(2):
            rows = pl.ds(b * 16, 16)
            copies.append((fem_hbm.at[b, :, p, :], basis.at[p, rows, pl.ds(0, LOCAL)]))
            copies.append((bem_hbm.at[b, :, p, :], basis.at[p, rows, pl.ds(LOCAL, PIECE)]))
    copies.append((w_hbm, image))
    copies = [pltpu.make_async_copy(a, b, in_sem.at[i]) for i, (a, b) in enumerate(copies)]
    for copy in copies:
        copy.start()

    total = sums[:8, :]
    for g in range(4):
        pack_q[8 * g : 8 * g + 8, :] = total if g == 0 else pltpu.roll(total, 128 - 32 * g, 1)
    gram_q = pack_q[:, :32]
    total = sums[8:, :]
    for g in range(6):
        pack[8 * g : 8 * g + 8, :] = total if g == 0 else pltpu.roll(total, 128 - 16 * g, 1)
    one = pack[:32, :16]
    norm = pack[32:48, :16]

    both = 2.0 * one - small_dot(gram_q, one, ((1,), (0,)))
    hess[...] = both
    left = small_dot(gram_q, both, ((1,), (0,))) - one
    gram = norm + small_dot(both, left, ((0,), (0,))) - small_dot(one, both, ((0,), (0,)))
    row_id = lax.broadcasted_iota(jnp.int32, (16, 16), 0)
    col_id = lax.broadcasted_iota(jnp.int32, (16, 16), 1)
    work = (gram + gram.T) * 0.5
    inverse = (row_id == col_id).astype(F32)
    upper = jnp.zeros((16, 16), F32)
    lower_inv = jnp.zeros((16, 16), F32)
    for j in range(16):
        pivot = work[j : j + 1, j : j + 1]
        root = lax.rsqrt(pivot)
        root = root * (1.5 - 0.5 * pivot * root * root)
        line = jnp.broadcast_to(work[j : j + 1, :] * root, (16, 16))
        line_inv = jnp.broadcast_to(inverse[j : j + 1, :] * root, (16, 16))
        column = jnp.broadcast_to(work[:, j : j + 1] * root, (16, 16))
        upper = jnp.where((row_id == j) & (col_id >= j), line, upper)
        lower_inv = jnp.where(row_id == j, line_inv, lower_inv)
        work = work - column * line
        inverse = inverse - column * line_inv
    rfac[...] = upper

    weights = -small_dot(lower_inv, both, ((1,), (1,)))
    w_pair = jnp.concatenate(split2(weights), axis=0)
    l_pair = jnp.concatenate(split2(lower_inv), axis=0)
    for copy in copies:
        copy.wait()
    leaving = []
    for p in range(2):
        q_high, q_low = split2(basis[p])
        i_high, i_low = split2(image[p * 16 : p * 16 + 16, :])
        first = jnp.dot(w_pair, q_high, preferred_element_type=F32)
        first = first + jnp.dot(l_pair, i_high, preferred_element_type=F32)
        second = jnp.dot(w_pair[:16], q_low, preferred_element_type=F32)
        second = second + jnp.dot(l_pair[:16], i_low, preferred_element_type=F32)
        made = first[:16] + first[16:] + second
        fem_out[p] = made[:, :LOCAL]
        bem_out[p] = made[:, LOCAL:]
        leaving.append(pltpu.make_async_copy(fem_out.at[p], next_fem.at[:, p, :], out_sem.at[p]))
        leaving.append(
            pltpu.make_async_copy(bem_out.at[p], next_bem.at[:, p, :], out_sem.at[2 + p])
        )
        leaving[-2].start()
        leaving[-1].start()
    for copy in leaving:
        copy.wait()


def body(fem_basis, bem_basis, diag, vals, cols, halo, mat, trace, slot):
    vmem = pl.BlockSpec(memory_space=pltpu.VMEM)
    hbm = pl.BlockSpec(memory_space=pl.ANY)
    dma = pltpu.SemaphoreType.DMA
    image, sums = pl.pallas_call(
        step_kernel,
        out_shape=(
            jax.ShapeDtypeStruct((VEC, WIDE), F32),
            jax.ShapeDtypeStruct((16, 128), F32),
        ),
        in_specs=[hbm] * 9,
        out_specs=(hbm, vmem),
        scratch_shapes=[
            pltpu.VMEM((2, VEC, LOCAL), F32),
            pltpu.VMEM((2, VEC, PIECE), F32),
            pltpu.VMEM((1, LOCAL), F32),
            pltpu.VMEM((16, LOCAL), F32),
            pltpu.VMEM((16, LOCAL), jnp.int32),
            pltpu.VMEM((4, 128), jnp.int32),
            pltpu.VMEM((1, 256), jnp.int32),
            pltpu.VMEM((1, PIECE), jnp.int32),
            dma((20,)),
            dma,
            pltpu.VMEM((512, 256), BF16),
            pltpu.VMEM((128, 256), BF16),
            pltpu.VMEM((4, VEC, 128), F32),
            pltpu.VMEM((4, VEC, 128), F32),
            pltpu.VMEM((VEC, ROWS * PIECE), BF16),
            pltpu.VMEM((COLS, VEC, PIECE), F32),
            pltpu.VMEM((COLS, VEC, PIECE), F32),
            pltpu.VMEM((DEVICES, 128), F32),
            pltpu.VMEM((ROWS, COLS, 128), F32),
            pltpu.VMEM((ROWS, COLS, 128), F32),
            pltpu.VMEM((2, 2048, 1024), BF16),
            pltpu.VMEM((VEC, WIDE), F32),
            pltpu.VMEM((2, 144, WIDE), BF16),
            pltpu.VMEM((48, 128), F32),
            pltpu.VMEM((2, 8, 128), F32),
            pltpu.VMEM((2, COLS, 8, 128), F32),
            pltpu.VMEM((2, ROWS, 8, 128), F32),
            dma((8,)),
            dma((4,)),
            dma((4,)),
            dma, dma, dma, dma, dma, dma, dma, dma,
            dma((2,)), dma((2,)), dma((2,)), dma((2,)),
        ],
        compiler_params=pltpu.CompilerParams(
            has_side_effects=True, collective_id=0, vmem_limit_bytes=60 << 20
        ),
    )(fem_basis, bem_basis, diag.reshape(1, LOCAL), vals, cols, halo, mat, trace.reshape(1, 256), slot.reshape(1, PIECE))
    next_fem, next_bem, hess, rfac = pl.pallas_call(
        finish_kernel,
        out_shape=(
            jax.ShapeDtypeStruct((16, 2, LOCAL), F32),
            jax.ShapeDtypeStruct((16, 2, PIECE), F32),
            jax.ShapeDtypeStruct((VEC, 16), F32),
            jax.ShapeDtypeStruct((16, 16), F32),
        ),
        in_specs=[hbm, hbm, hbm, vmem],
        out_specs=(hbm, hbm, vmem, vmem),
        scratch_shapes=[
            pltpu.VMEM((2, VEC, WIDE), F32),
            pltpu.VMEM((VEC, WIDE), F32),
            pltpu.VMEM((VEC, 128), F32),
            pltpu.VMEM((48, 128), F32),
            pltpu.VMEM((2, 16, LOCAL), F32),
            pltpu.VMEM((2, 16, PIECE), F32),
            dma((9,)),
            dma((4,)),
        ],
        compiler_params=pltpu.CompilerParams(vmem_limit_bytes=60 << 20),
    )(fem_basis, bem_basis, image, sums)
    return next_fem, next_bem, hess.reshape(2, 16, 16), rfac


def solution(mesh):
    both = ("row", "col")
    return jax.shard_map(
        body,
        mesh=mesh,
        in_specs=(
            P(None, None, None, both), P(None, None, None, both), P(both), P(None, both),
            P(None, both), P(None, both), P(None, "row", "col"), P(both), P(both),
        ),
        out_specs=(P(None, None, both), P(None, None, both), P(), P()),
        check_vma=False,
    )
```

time: 66.8 us -> 42.3 us (0.63)
  local copies, waits for them, and re-layouts: 12.7 us -> 0 us
  Pallas kernels: 53 us -> 41.5 us
    pallas_call x1 -> x2, Pallas kernels: 53 us -> 41.5 us  [the longest x1 36.6 us: body(): pl.pallas_call(step_kernel, out_shape=(jax.ShapeDtypeStruct((VEC, WIDE),...]
    unnamed x18 -> x0, local copies, waits for them, and re-layouts: 10.6 us -> none
    transpose x2 -> x0, local copies, waits for them, and re-layouts: 2.11 us -> none  [the longest x1 1.35 us: body(): fem = jnp.transpose(fem_basis, (0, 2, 1, 3)).reshape(2, VEC, LOCAL)]
where the time goes in v2:
time: 42.3 us; the launch traced here: 42.1 us
  Pallas kernels  41.5 us (98%)
  between operations  0.64 us (2%)
    pallas_call x1, Pallas kernels, body(): pl.pallas_call(step_kernel, out_shape=(jax.ShapeDtypeStruct((VEC, WIDE),...  36.6 us
    pallas_call x1, Pallas kernels, body(): pl.pallas_call(finish_kernel, out_shape=(jax.ShapeDtypeStruct((16, 2, LOC...  4.91 us

profile of v2, /device:TPU:1, one launch (start us, length us, event | category | flops | bytes accessed | tf_op | source)
XLA Modules:
  0.0 42.1 jit_solution(10981633912646717564)
XLA Ops:
  0.6 36.6 %shard_map.120 = (f32[32,2176]{1,0:T(8,128)}, f32[16,128]{1,0:T(8,128)}) custom-call(f32[2,16,2,2048]{3,2,1,0:T(2,128)} %fem_hbm.3, f32[2,16,2,128]{3,2,1,0:T(2,128)} %bem_hbm.3, f32[1,2048]{1,0:T(1,128)} %bitcast.4, f32[16,2048]{1,0:T(8,128)} %vals_hbm.1, s32[16,2048]{1,0:T(8,128)} %cols_hbm.1, s32[4,128]{1,0:T(4,128)} %halo_hbm.1, ...), custom_call_target="tpu_custom_call" | custom-call | tf_op jit(solution)/shard_map/pallas_call | solution.py:511
  37.2 4.9 %shard_map.121 = (f32[16,2,2048]{2,1,0:T(2,128)}, f32[16,2,128]{2,1,0:T(2,128)}, f32[32,16]{1,0:T(8,128)}, f32[16,16]{1,0:T(8,128)}) custom-call(f32[2,16,2,2048]{3,2,1,0:T(2,128)} %fem_hbm.3, f32[2,16,2,128]{3,2,1,0:T(2,128)} %bem_hbm.3, f32[32,2176]{1,0:T(8,128)} %get-tuple-element.10.w_hbm, f32[16,128]{1,0:T(8,128)} %get-tuple-element.11.sums), custom_call_target="tpu_custom_call" | custom-call | tf_op jit(solution)/shard_map/pallas_call | solution.py:557

commit v3 on v2

--- a/solution.py
+++ b/solution.py
@@ -19,8 +19,9 @@
 WIDE = LOCAL + PIECE
 COUNT = 2.0 * DEVICES * (LOCAL + PIECE)
 NT = (((1,), (1,)), ((), ()))
-BY_LANE_NEAR = (1, 4, 7, 10, 13)
-BY_LANE_FAR = (1, 3, 5, 7, 9, 11, 13)
+BY_LANE_NEAR = (1, 3, 5, 7, 9, 11, 13, 15)
+BY_LANE_FAR = (1, 3, 5, 7, 9, 11, 13, 15)
+BY_LANE_ALL = (1, 3, 5, 7, 9, 11, 13, 15)
 FIRST_CHUNKS = 4
 
 
@@ -44,17 +45,24 @@
     return lax.dot_general(a, b, (dims, ((), ())), precision=HIGHEST, preferred_element_type=F32)
 
 
+def paired(x):
+    top = jnp.maximum(jnp.max(jnp.abs(x), axis=1, keepdims=True), 1e-30)
+    whole = jnp.round(x * (32000.0 / top)).astype(jnp.int32)
+    return (whole[:16] << 16) | (whole[16:] & 0xFFFF), top * (1.0 / 32000.0)
+
+
 def looked_up(table, column, tiles, first):
     halves = []
     for half in range(2):
-        here = jnp.broadcast_to(column[:, half * 128 : half * 128 + 128], (VEC, 128))
+        here = jnp.broadcast_to(column[:, half * 128 : half * 128 + 128], (16, 128))
         low = here & 127
         high = here >> 7
-        got = jnp.zeros((VEC, 128), F32)
+        got = jnp.zeros((16, 128), jnp.int32)
         for t in range(tiles):
             got = jnp.where(high == t + first, lane_gather(table(t), low), got)
         halves.append(got)
-    return jnp.concatenate(halves, axis=1)
+    got = jnp.concatenate(halves, axis=1)
+    return jnp.concatenate([got >> 16, (got << 16) >> 16], axis=0).astype(F32)
 
 
 def multiplied_up(pieces, column, tiles, first):
@@ -78,7 +86,7 @@
     fem_hbm, bem_hbm, diag_hbm, vals_hbm, cols_hbm, halo_hbm, mat, trace_hbm, slot_hbm,
     w_hbm, sums,
     fem, bem, diag, vals, cols, halo, trace, slot, in_sem, out_sem,
-    near, far, halo_out, halo_in, phi, partial, arrived, swap_out, swap_mid, swap_in,
+    near, pairs, unit, halo_out, halo_in, phi, partial, arrived, swap_out, swap_mid, swap_in,
     mat_buf, image, zp, pack, sum_out, col_in, row_in,
     mat_sem, halo_send, halo_recv, phi_send, phi_recv, part_send, part_recv,
     mid_send, mid_recv, swap_send, swap_recv, col_send, col_recv, row_send, row_recv,
@@ -168,6 +176,29 @@
         @pl.when(missing)
         def _(d=d):
             halo_in[d] = jnp.zeros((VEC, 128), F32)
+
+    pl.semaphore_wait(barrier, ROWS + COLS - 2)
+
+    def send_phi(k, _):
+        other = lax.rem(r + k, ROWS)
+        remote(phi.at[:, mine], phi.at[:, mine], phi_send, phi_recv, other, c).start()
+        return 0
+
+    lax.fori_loop(1, ROWS, send_phi, 0)
+
+    neighbours = (
+        (c + 1 < COLS, r, c + 1, c > 0),
+        (c > 0, r, c - 1, c + 1 < COLS),
+        (r + 1 < ROWS, r + 1, c, r > 0),
+        (r > 0, r - 1, c, r + 1 < ROWS),
+    )
+    for d, (exists, row, col, _) in enumerate(neighbours):
+
+        @pl.when(exists)
+        def _(d=d, row=row, col=col):
+            remote(
+                halo_out.at[d], halo_in.at[d], halo_send.at[d], halo_recv.at[d], row, col
+            ).start()
 
     lane = lax.broadcasted_iota(jnp.int32, (8, 128), 1)
     trace_lo = jnp.broadcast_to(trace[:, :128], (8, 128))
@@ -187,49 +218,6 @@
     back = back[:VEC] + back[VEC : 2 * VEC] + back[2 * VEC :]
     swap_out[...] = jnp.concatenate(leaving + [back[:, :128], back[:, 128:]], axis=0).T
 
-    for t in range(8):
-        for a, piece in enumerate(split2(fem[1, :, t * 256 : (t + 1) * 256])):
-            near[a * 256 + t * 32 : a * 256 + t * 32 + 32, :] = piece
-    ready("sparse")
-
-    def product_near(j, _):
-        here = pl.ds(pl.multiple_of(j * 256, 256), 256)
-        acc = diag[:, here] * fem[1, :, here]
-        for k in range(16):
-            column = cols[k : k + 1, here]
-            if k in BY_LANE_NEAR:
-                got = looked_up(lambda t: fem[1, :, t * 128 : (t + 1) * 128], column, 16, 0)
-            else:
-                got = multiplied_up(near[...], column, 8, 0)
-            acc = acc + vals[k : k + 1, here] * got
-        image[:, here] = acc
-        return 0
-
-    lax.fori_loop(0, FIRST_CHUNKS, product_near, 0)
-
-    pl.semaphore_wait(barrier, ROWS + COLS - 2)
-
-    def send_phi(k, _):
-        other = lax.rem(r + k, ROWS)
-        remote(phi.at[:, mine], phi.at[:, mine], phi_send, phi_recv, other, c).start()
-        return 0
-
-    lax.fori_loop(1, ROWS, send_phi, 0)
-
-    neighbours = (
-        (c + 1 < COLS, r, c + 1, c > 0),
-        (c > 0, r, c - 1, c + 1 < COLS),
-        (r + 1 < ROWS, r + 1, c, r > 0),
-        (r > 0, r - 1, c, r + 1 < ROWS),
-    )
-    for d, (exists, row, col, _) in enumerate(neighbours):
-
-        @pl.when(exists)
-        def _(d=d, row=row, col=col):
-            remote(
-                halo_out.at[d], halo_in.at[d], halo_send.at[d], halo_recv.at[d], row, col
-            ).start()
-
     def send_mid(k, _):
         other = lax.rem(r + k, ROWS)
         block = pl.ds(pl.multiple_of(other * COLS, COLS), COLS)
@@ -239,7 +227,82 @@
     lax.fori_loop(1, ROWS, send_mid, 0)
     swap_mid[r] = swap_out[pl.ds(pl.multiple_of(r * COLS, COLS), COLS)]
 
-    lax.fori_loop(FIRST_CHUNKS, LOCAL // 256, product_near, 0)
+    ready("old")
+    for p in range(2):
+        rows = slice(p * 16, p * 16 + 16)
+        for b in range(2):
+            for a, x in enumerate(split2(fem[b, rows, :])):
+                zp[p, a * 48 + b * 16 : a * 48 + b * 16 + 16, :LOCAL] = x
+            for a, x in enumerate(split2(bem[b, rows, :])):
+                zp[p, a * 48 + b * 16 : a * 48 + b * 16 + 16, LOCAL:] = x
+    own = jnp.zeros((VEC, VEC), F32)
+    for p in range(2):
+        whole = jnp.concatenate([zp[p, :32, :], zp[p, 48:80, :]], axis=0)
+        for b in range(2):
+            both = lax.dot_general(
+                whole, zp[p, b * 48 : b * 48 + 32, :], NT, preferred_element_type=F32
+            )
+            own = own + both[:32] + both[32:]
+    pack[...] = jnp.zeros((48, 128), F32)
+    pack[:32, :32] = own
+    packed = pack[0:8, :]
+    for g in range(1, 4):
+        packed = packed + pltpu.roll(pack[8 * g : 8 * g + 8, :], 32 * g, 1)
+    sum_out[8:, :] = packed
+
+    for t in range(8):
+        for a, piece in enumerate(split2(fem[1, :, t * 256 : (t + 1) * 256])):
+            near[a * 320 + t * 32 : a * 320 + t * 32 + 32, :] = piece
+    pairs[:, :LOCAL], unit[...] = paired(fem[1])
+    ready("sparse")
+
+    def product(j, where, tiles, first, by_lane, start):
+        here = pl.ds(pl.multiple_of(j * 256, 256), 256)
+        acc = start(here)
+        lane_acc = jnp.zeros((VEC, 256), F32)
+        high = where[first * VEC : (first + tiles) * VEC, :]
+        low = where[(10 + first) * VEC : (10 + first + tiles) * VEC, :]
+        pieces = jnp.concatenate([high, low], axis=0)
+        for k in range(16):
+            column = cols[k : k + 1, here]
+            value = vals[k : k + 1, here]
+            if k in by_lane:
+                got = looked_up(
+                    lambda t: pairs[:, (2 * first + t) * 128 : (2 * first + t + 1) * 128],
+                    column, 2 * tiles, 2 * first,
+                )
+                lane_acc = lane_acc + value * got
+            else:
+                acc = acc + value * multiplied_up(pieces, column, tiles, first)
+        image[:, here] = acc + lane_acc * unit[...]
+        return 0
+
+    def diagonal(here):
+        return diag[:, here] * fem[1, :, here]
+
+    def product_near(j, _):
+        return product(j, near, 8, 0, BY_LANE_NEAR, diagonal)
+
+    def product_far(j, _):
+        return product(j, near, 2, 8, BY_LANE_FAR, lambda here: image[:, here])
+
+    def product_all(j, _):
+        return product(j, near, 10, 0, BY_LANE_ALL, diagonal)
+
+    lax.fori_loop(0, FIRST_CHUNKS, product_near, 0)
+
+    wait_bytes(swap_mid.at[pl.ds(0, ROWS - 1)], mid_recv)
+
+    def send_swap(k, _):
+        other = lax.rem(c + k, COLS)
+        remote(
+            swap_mid.at[:, pl.ds(other, 1), :], swap_in.at[:, pl.ds(c, 1), :],
+            swap_send, swap_recv, r, other,
+        ).start()
+        return 0
+
+    lax.fori_loop(1, COLS, send_swap, 0)
+    swap_in[:, pl.ds(c, 1), :] = swap_mid[:, pl.ds(c, 1), :]
 
     wait_bytes(phi.at[:, pl.ds(0, (ROWS - 1) * PIECE)], phi_recv)
     phi_all = phi[...]
@@ -264,74 +327,36 @@
     lax.fori_loop(0, 8, multiply, 0)
     arrived[c] = partial[c]
 
-    wait_bytes(swap_mid.at[pl.ds(0, ROWS - 1)], mid_recv)
-
-    def send_swap(k, _):
-        other = lax.rem(c + k, COLS)
-        remote(
-            swap_mid.at[:, pl.ds(other, 1), :], swap_in.at[:, pl.ds(c, 1), :],
-            swap_send, swap_recv, r, other,
-        ).start()
-        return 0
-
-    lax.fori_loop(1, COLS, send_swap, 0)
-    swap_in[:, pl.ds(c, 1), :] = swap_mid[:, pl.ds(c, 1), :]
-
-    ready("old")
-    for p in range(2):
-        for b in range(2):
-            rows = slice(p * 16, p * 16 + 16)
-            for a, x in enumerate(split3(fem[b, rows, :])):
-                zp[p, a * 48 + b * 16 : a * 48 + b * 16 + 16, :LOCAL] = x
-            for a, x in enumerate(split3(bem[b, rows, :])):
-                zp[p, a * 48 + b * 16 : a * 48 + b * 16 + 16, LOCAL:] = x
-    own = jnp.zeros((VEC, VEC), F32)
-    for p in range(2):
-        whole = jnp.concatenate([zp[p, a * 48 : a * 48 + 32, :] for a in range(3)], axis=0)
-        for b in range(3):
-            both = lax.dot_general(
-                whole, zp[p, b * 48 : b * 48 + 32, :], NT, preferred_element_type=F32
-            )
-            own = own + both[:32] + both[32:64] + both[64:]
-    pack[...] = jnp.zeros((48, 128), F32)
-    pack[:32, :32] = own
-    packed = pack[0:8, :]
-    for g in range(1, 4):
-        packed = packed + pltpu.roll(pack[8 * g : 8 * g + 8, :], 32 * g, 1)
-    sum_out[0] = packed
-
-    def reduce_cols(n):
-        col_in[n, c] = sum_out[n]
+    def reduce_cols():
+        col_in[c] = sum_out[...]
 
         def send(k, _):
             other = lax.rem(c + k, COLS)
-            remote(sum_out.at[n], col_in.at[n, c], col_send.at[n], col_recv.at[n], r, other).start()
+            remote(sum_out, col_in.at[c], col_send, col_recv, r, other).start()
             return 0
 
         lax.fori_loop(1, COLS, send, 0)
 
-    def reduce_rows(n):
-        wait_bytes(col_in.at[n, pl.ds(0, COLS - 1)], col_recv.at[n])
-        total = col_in[n, 0]
+    def reduce_rows():
+        wait_bytes(col_in.at[pl.ds(0, COLS - 1)], col_recv)
+        total = col_in[0]
         for k in range(1, COLS):
-            total = total + col_in[n, k]
-        row_in[n, r] = total
+            total = total + col_in[k]
+        row_in[r] = total
 
         def send(k, _):
             other = lax.rem(r + k, ROWS)
-            remote(row_in.at[n, r], row_in.at[n, r], row_send.at[n], row_recv.at[n], other, c).start()
+            remote(row_in.at[r], row_in.at[r], row_send, row_recv, other, c).start()
             return 0
 
         lax.fori_loop(1, ROWS, send, 0)
 
-    def reduced(n):
-        wait_bytes(row_in.at[n, pl.ds(0, ROWS - 1)], row_recv.at[n])
-        total = row_in[n, 0]
+    def reduced():
+        wait_bytes(row_in.at[pl.ds(0, ROWS - 1)], row_recv)
+        total = row_in[0]
         for k in range(1, ROWS):
-            total = total + row_in[n, k]
+            total = total + row_in[k]
         return total * (1.0 / COUNT)
-
-    reduce_cols(0)
 
     for d, (_, _, _, comes) in enumerate(neighbours):
 
@@ -339,26 +364,13 @@
         def _(d=d):
             wait_bytes(halo_in.at[d], halo_recv.at[d])
 
+    outer = jnp.concatenate([halo_in[d] for d in range(4)], axis=1)
     for t in range(2):
-        x = jnp.concatenate([halo_in[2 * t], halo_in[2 * t + 1]], axis=1)
-        for a, piece in enumerate(split2(x)):
-            far[a * 64 + t * 32 : a * 64 + t * 32 + 32, :] = piece
-
-    def product_far(j, _):
-        here = pl.ds(pl.multiple_of(j * 256, 256), 256)
-        acc = image[:, here]
-        for k in range(16):
-            column = cols[k : k + 1, here]
-            if k in BY_LANE_FAR:
-                got = looked_up(lambda t: halo_in[t], column, 4, 16)
-            else:
-                got = multiplied_up(far[...], column, 2, 8)
-            acc = acc + vals[k : k + 1, here] * got
-        image[:, here] = acc
-        return 0
-
-    lax.fori_loop(0, LOCAL // 256, product_far, 0)
-    reduce_rows(0)
+        for a, piece in enumerate(split2(outer[:, t * 256 : t * 256 + 256])):
+            near[a * 320 + 256 + t * 32 : a * 320 + 288 + t * 32, :] = piece
+    pairs[...], unit[...] = paired(jnp.concatenate([fem[1], outer], axis=1))
+    lax.fori_loop(0, FIRST_CHUNKS, product_far, 0)
+    lax.fori_loop(FIRST_CHUNKS, LOCAL // 256, product_all, 0)
 
     wait_bytes(swap_in.at[:, pl.ds(0, COLS - 1), :], swap_recv)
     met = swap_in[...].reshape(DEVICES, 128).T
@@ -376,19 +388,19 @@
         here = slice(t * 256, t * 256 + 256)
         image[:, here] = image[:, here] + put[:32] + put[32:64] + put[64:]
     for p in range(2):
-        for a, x in enumerate(split3(image[p * 16 : p * 16 + 16, :LOCAL])):
+        for a, x in enumerate(split2(image[p * 16 : p * 16 + 16, :LOCAL])):
             zp[p, a * 48 + 32 : a * 48 + 48, :LOCAL] = x
 
     def inner(columns):
         made = jnp.zeros((48, 16), F32)
         for p in range(2):
             whole = zp[p, :, columns]
-            for b in range(3):
+            for b in range(2):
                 both = lax.dot_general(
                     whole, zp[p, b * 48 + 32 : b * 48 + 48, columns], NT,
                     preferred_element_type=F32,
                 )
-                made = made + both[:48] + both[48:96] + both[96:]
+                made = made + both[:48] + both[48:]
         return made
 
     pack[...] = jnp.zeros((48, 128), F32)
@@ -399,17 +411,16 @@
         bem_image = bem_image + arrived[k]
     image[:, LOCAL:] = bem_image
     for p in range(2):
-        for a, x in enumerate(split3(bem_image[p * 16 : p * 16 + 16, :])):
+        for a, x in enumerate(split2(bem_image[p * 16 : p * 16 + 16, :])):
             zp[p, a * 48 + 32 : a * 48 + 48, LOCAL:] = x
     pack[:, :16] = pack[:, :16] + inner(slice(LOCAL, WIDE))
     packed = pack[0:8, :]
     for g in range(1, 6):
         packed = packed + pltpu.roll(pack[8 * g : 8 * g + 8, :], 16 * g, 1)
-    sum_out[1] = packed
-    reduce_cols(1)
+    sum_out[:8, :] = packed
+    reduce_cols()
     leave = pltpu.make_async_copy(image, w_hbm, out_sem)
     leave.start()
-    sums[:8, :] = reduced(0)
 
     for d, (exists, _, _, _) in enumerate(neighbours):
 
@@ -421,13 +432,11 @@
     wait_bytes(arrived.at[pl.ds(0, COLS - 1)], part_send)
     wait_bytes(swap_mid.at[pl.ds(0, ROWS - 1)], mid_send)
     wait_bytes(swap_in.at[:, pl.ds(0, COLS - 1), :], swap_send)
-    wait_bytes(col_in.at[0, pl.ds(0, COLS - 1)], col_send.at[0])
-    wait_bytes(row_in.at[0, pl.ds(0, ROWS - 1)], row_send.at[0])
-    reduce_rows(1)
-    wait_bytes(col_in.at[1, pl.ds(0, COLS - 1)], col_send.at[1])
+    reduce_rows()
+    wait_bytes(col_in.at[pl.ds(0, COLS - 1)], col_send)
     leave.wait()
-    sums[8:, :] = reduced(1)
-    wait_bytes(row_in.at[1, pl.ds(0, ROWS - 1)], row_send.at[1])
+    sums[...] = reduced()
+    wait_bytes(row_in.at[pl.ds(0, ROWS - 1)], row_send)
 
 
 def finish_kernel(
@@ -445,11 +454,11 @@
     for copy in copies:
         copy.start()
 
-    total = sums[:8, :]
+    total = sums[8:, :]
     for g in range(4):
         pack_q[8 * g : 8 * g + 8, :] = total if g == 0 else pltpu.roll(total, 128 - 32 * g, 1)
     gram_q = pack_q[:, :32]
-    total = sums[8:, :]
+    total = sums[:8, :]
     for g in range(6):
         pack[8 * g : 8 * g + 8, :] = total if g == 0 else pltpu.roll(total, 128 - 16 * g, 1)
     one = pack[:32, :16]
@@ -527,8 +536,9 @@
             pltpu.VMEM((1, PIECE), jnp.int32),
             dma((20,)),
             dma,
-            pltpu.VMEM((512, 256), BF16),
-            pltpu.VMEM((128, 256), BF16),
+            pltpu.VMEM((640, 256), BF16),
+            pltpu.VMEM((16, 2560), jnp.int32),
+            pltpu.VMEM((VEC, 1), F32),
             pltpu.VMEM((4, VEC, 128), F32),
             pltpu.VMEM((4, VEC, 128), F32),
             pltpu.VMEM((VEC, ROWS * PIECE), BF16),
@@ -539,16 +549,16 @@
             pltpu.VMEM((ROWS, COLS, 128), F32),
             pltpu.VMEM((2, 2048, 1024), BF16),
             pltpu.VMEM((VEC, WIDE), F32),
-            pltpu.VMEM((2, 144, WIDE), BF16),
+            pltpu.VMEM((2, 96, WIDE), BF16),
             pltpu.VMEM((48, 128), F32),
-            pltpu.VMEM((2, 8, 128), F32),
-            pltpu.VMEM((2, COLS, 8, 128), F32),
-            pltpu.VMEM((2, ROWS, 8, 128), F32),
+            pltpu.VMEM((16, 128), F32),
+            pltpu.VMEM((COLS, 16, 128), F32),
+            pltpu.VMEM((ROWS, 16, 128), F32),
             dma((8,)),
             dma((4,)),
             dma((4,)),
             dma, dma, dma, dma, dma, dma, dma, dma,
-            dma((2,)), dma((2,)), dma((2,)), dma((2,)),
+            dma, dma, dma, dma,
         ],
         compiler_params=pltpu.CompilerParams(
             has_side_effects=True, collective_id=0, vmem_limit_bytes=60 << 20

time: 42.3 us -> 37.8 us (0.89)
  Pallas kernels: 41.5 us -> 37 us
    pallas_call x1, Pallas kernels: 36.6 us -> 32.1 us  [body(): pl.pallas_call(step_kernel, out_shape=(jax.ShapeDtypeStruct((VEC, WIDE),...]
where the time goes in v3:
time: 37.8 us; the launch traced here: 37.7 us
  Pallas kernels  37 us (98%)
  between operations  0.64 us (2%)
    pallas_call x1, Pallas kernels, body(): pl.pallas_call(step_kernel, out_shape=(jax.ShapeDtypeStruct((VEC, WIDE),...  32.1 us
    pallas_call x1, Pallas kernels, body(): pl.pallas_call(finish_kernel, out_shape=(jax.ShapeDtypeStruct((16, 2, LOC...  4.92 us

profile of v3, /device:TPU:1, one launch (start us, length us, event | category | flops | bytes accessed | tf_op | source)
XLA Modules:
  0.0 37.7 jit_solution(16378838629074261807)
XLA Ops:
  0.6 32.1 %shard_map.120 = (f32[32,2176]{1,0:T(8,128)}, f32[16,128]{1,0:T(8,128)}) custom-call(f32[2,16,2,2048]{3,2,1,0:T(2,128)} %fem_hbm.3, f32[2,16,2,128]{3,2,1,0:T(2,128)} %bem_hbm.3, f32[1,2048]{1,0:T(1,128)} %bitcast.4, f32[16,2048]{1,0:T(8,128)} %vals_hbm.1, s32[16,2048]{1,0:T(8,128)} %cols_hbm.1, s32[4,128]{1,0:T(4,128)} %halo_hbm.1, ...), custom_call_target="tpu_custom_call" | custom-call | tf_op jit(solution)/shard_map/pallas_call | solution.py:520
  32.7 4.9 %shard_map.121 = (f32[16,2,2048]{2,1,0:T(2,128)}, f32[16,2,128]{2,1,0:T(2,128)}, f32[32,16]{1,0:T(8,128)}, f32[16,16]{1,0:T(8,128)}) custom-call(f32[2,16,2,2048]{3,2,1,0:T(2,128)} %fem_hbm.3, f32[2,16,2,128]{3,2,1,0:T(2,128)} %bem_hbm.3, f32[32,2176]{1,0:T(8,128)} %get-tuple-element.10.w_hbm, f32[16,128]{1,0:T(8,128)} %get-tuple-element.11.sums), custom_call_target="tpu_custom_call" | custom-call | tf_op jit(solution)/shard_map/pallas_call | solution.py:567

commit v4 on v3

--- a/solution.py
+++ b/solution.py
@@ -23,6 +23,11 @@
 BY_LANE_FAR = (1, 3, 5, 7, 9, 11, 13, 15)
 BY_LANE_ALL = (1, 3, 5, 7, 9, 11, 13, 15)
 FIRST_CHUNKS = 4
+FAR_FIRST = (
+    (2, 2), (2, 1), (2, 3), (1, 2), (3, 2), (2, 0), (0, 2), (1, 1), (1, 3), (3, 1), (3, 3),
+    (1, 0), (3, 0), (0, 1), (0, 3),
+)
+ROW_STEPS = (4, 5, 3, 2, 6, 7, 1)
 
 
 def split2(x):
@@ -84,7 +89,7 @@
 
 def step_kernel(
     fem_hbm, bem_hbm, diag_hbm, vals_hbm, cols_hbm, halo_hbm, mat, trace_hbm, slot_hbm,
-    w_hbm, sums,
+    z_hbm, sums,
     fem, bem, diag, vals, cols, halo, trace, slot, in_sem, out_sem,
     near, pairs, unit, halo_out, halo_in, phi, partial, arrived, swap_out, swap_mid, swap_in,
     mat_buf, image, zp, pack, sum_out, col_in, row_in,
@@ -137,8 +142,13 @@
     load("sparse", [(cols_hbm, cols), (vals_hbm, vals), (diag_hbm, diag)])
     load("old", parts(fem_hbm, fem, (0,)))
 
+    def chunk_at(k):
+        y = lax.rem(c // 4 + 2 + 3 * (k // 2), 4)
+        x = lax.rem(lax.rem(c, 4) // 2 + 1 + lax.rem(k, 2), 2)
+        return 2 * y + x
+
     def matrix_copy(k):
-        chunk = lax.rem(k + c // 2, 8)
+        chunk = chunk_at(k)
         rows = pl.ds(pl.multiple_of(chunk * 256, 256), 256)
         return pltpu.make_async_copy(mat.at[:, rows, :], mat_buf.at[:, rows, :], mat_sem.at[k])
 
@@ -179,12 +189,9 @@
 
     pl.semaphore_wait(barrier, ROWS + COLS - 2)
 
-    def send_phi(k, _):
+    for k in ROW_STEPS:
         other = lax.rem(r + k, ROWS)
         remote(phi.at[:, mine], phi.at[:, mine], phi_send, phi_recv, other, c).start()
-        return 0
-
-    lax.fori_loop(1, ROWS, send_phi, 0)
 
     neighbours = (
         (c + 1 < COLS, r, c + 1, c > 0),
@@ -218,14 +225,19 @@
     back = back[:VEC] + back[VEC : 2 * VEC] + back[2 * VEC :]
     swap_out[...] = jnp.concatenate(leaving + [back[:, :128], back[:, 128:]], axis=0).T
 
-    def send_mid(k, _):
+    for k in ROW_STEPS:
         other = lax.rem(r + k, ROWS)
         block = pl.ds(pl.multiple_of(other * COLS, COLS), COLS)
         remote(swap_out.at[block], swap_mid.at[r], mid_send, mid_recv, other, c).start()
-        return 0
-
-    lax.fori_loop(1, ROWS, send_mid, 0)
     swap_mid[r] = swap_out[pl.ds(pl.multiple_of(r * COLS, COLS), COLS)]
+
+    def gathered(groups, width):
+        made = jnp.zeros((8, 128), F32)
+        for g in range(groups):
+            x = pack[8 * g : 8 * g + 8, :]
+            x = jnp.where(lane < width, x + pltpu.roll(x, 128 - width, 1), 0.0)
+            made = made + (x if g == 0 else pltpu.roll(x, width * g, 1))
+        return made
 
     ready("old")
     for p in range(2):
@@ -235,20 +247,13 @@
                 zp[p, a * 48 + b * 16 : a * 48 + b * 16 + 16, :LOCAL] = x
             for a, x in enumerate(split2(bem[b, rows, :])):
                 zp[p, a * 48 + b * 16 : a * 48 + b * 16 + 16, LOCAL:] = x
-    own = jnp.zeros((VEC, VEC), F32)
+    own = jnp.zeros((2 * VEC, 2 * VEC), F32)
     for p in range(2):
         whole = jnp.concatenate([zp[p, :32, :], zp[p, 48:80, :]], axis=0)
-        for b in range(2):
-            both = lax.dot_general(
-                whole, zp[p, b * 48 : b * 48 + 32, :], NT, preferred_element_type=F32
-            )
-            own = own + both[:32] + both[32:]
+        own = own + lax.dot_general(whole, whole, NT, preferred_element_type=F32)
     pack[...] = jnp.zeros((48, 128), F32)
-    pack[:32, :32] = own
-    packed = pack[0:8, :]
-    for g in range(1, 4):
-        packed = packed + pltpu.roll(pack[8 * g : 8 * g + 8, :], 32 * g, 1)
-    sum_out[8:, :] = packed
+    pack[:32, :64] = own[:32] + own[32:]
+    sum_out[8:, :] = gathered(4, 32)
 
     for t in range(8):
         for a, piece in enumerate(split2(fem[1, :, t * 256 : (t + 1) * 256])):
@@ -293,15 +298,12 @@
 
     wait_bytes(swap_mid.at[pl.ds(0, ROWS - 1)], mid_recv)
 
-    def send_swap(k, _):
-        other = lax.rem(c + k, COLS)
+    for dy, dx in FAR_FIRST:
+        other = lax.rem(c // 4 + dy, 4) * 4 + lax.rem(c + dx, 4)
         remote(
             swap_mid.at[:, pl.ds(other, 1), :], swap_in.at[:, pl.ds(c, 1), :],
             swap_send, swap_recv, r, other,
         ).start()
-        return 0
-
-    lax.fori_loop(1, COLS, send_swap, 0)
     swap_in[:, pl.ds(c, 1), :] = swap_mid[:, pl.ds(c, 1), :]
 
     wait_bytes(phi.at[:, pl.ds(0, (ROWS - 1) * PIECE)], phi_recv)
@@ -309,7 +311,7 @@
     turned = jnp.concatenate([-phi_all[16:], phi_all[:16]], axis=0)
 
     def multiply(k, _):
-        chunk = lax.rem(k + c // 2, 8)
+        chunk = chunk_at(k)
         matrix_copy(k).wait()
         rows = pl.ds(pl.multiple_of(chunk * 256, 256), 256)
         out = lax.dot_general(phi_all, mat_buf[0, rows, :], NT, preferred_element_type=F32)
@@ -330,12 +332,9 @@
     def reduce_cols():
         col_in[c] = sum_out[...]
 
-        def send(k, _):
-            other = lax.rem(c + k, COLS)
+        for dy, dx in FAR_FIRST:
+            other = lax.rem(c // 4 + dy, 4) * 4 + lax.rem(c + dx, 4)
             remote(sum_out, col_in.at[c], col_send, col_recv, r, other).start()
-            return 0
-
-        lax.fori_loop(1, COLS, send, 0)
 
     def reduce_rows():
         wait_bytes(col_in.at[pl.ds(0, COLS - 1)], col_recv)
@@ -344,12 +343,9 @@
             total = total + col_in[k]
         row_in[r] = total
 
-        def send(k, _):
+        for k in ROW_STEPS:
             other = lax.rem(r + k, ROWS)
             remote(row_in.at[r], row_in.at[r], row_send, row_recv, other, c).start()
-            return 0
-
-        lax.fori_loop(1, ROWS, send, 0)
 
     def reduced():
         wait_bytes(row_in.at[pl.ds(0, ROWS - 1)], row_recv)
@@ -380,10 +376,11 @@
     )
     answers = jnp.concatenate([met[64:96], met[96:]], axis=1)
     answers = jnp.concatenate(split3(answers), axis=0)
-    targets = jnp.concatenate(trace_q, axis=1)
+    targets = jnp.concatenate(trace_q, axis=1).astype(jnp.int16)
+    targets = jnp.broadcast_to(targets, (256, 256))
     for t in range(LOCAL // 256):
-        row = lax.broadcasted_iota(jnp.int32, (256, 256), 0) + t * 256
-        hot = (row == targets).astype(F32).astype(BF16)
+        row = lax.broadcasted_iota(jnp.int16, (256, 256), 0) + jnp.int16(t * 256)
+        hot = jnp.where(row == targets, jnp.ones((256, 256), BF16), jnp.zeros((256, 256), BF16))
         put = lax.dot_general(answers, hot, NT, preferred_element_type=F32)
         here = slice(t * 256, t * 256 + 256)
         image[:, here] = image[:, here] + put[:32] + put[32:64] + put[64:]
@@ -392,34 +389,27 @@
             zp[p, a * 48 + 32 : a * 48 + 48, :LOCAL] = x
 
     def inner(columns):
-        made = jnp.zeros((48, 16), F32)
+        made = jnp.zeros((96, 32), F32)
         for p in range(2):
-            whole = zp[p, :, columns]
-            for b in range(2):
-                both = lax.dot_general(
-                    whole, zp[p, b * 48 + 32 : b * 48 + 48, columns], NT,
-                    preferred_element_type=F32,
-                )
-                made = made + both[:48] + both[48:]
-        return made
+            images = jnp.concatenate([zp[p, 32:48, columns], zp[p, 80:96, columns]], axis=0)
+            made = made + lax.dot_general(
+                zp[p, :, columns], images, NT, preferred_element_type=F32
+            )
+        return made[:48] + made[48:]
 
     pack[...] = jnp.zeros((48, 128), F32)
-    pack[:, :16] = inner(slice(0, LOCAL))
+    pack[:, :32] = inner(slice(0, LOCAL))
     wait_bytes(arrived.at[pl.ds(0, COLS - 1)], part_recv)
     bem_image = taken
     for k in range(COLS):
         bem_image = bem_image + arrived[k]
-    image[:, LOCAL:] = bem_image
     for p in range(2):
         for a, x in enumerate(split2(bem_image[p * 16 : p * 16 + 16, :])):
             zp[p, a * 48 + 32 : a * 48 + 48, LOCAL:] = x
-    pack[:, :16] = pack[:, :16] + inner(slice(LOCAL, WIDE))
-    packed = pack[0:8, :]
-    for g in range(1, 6):
-        packed = packed + pltpu.roll(pack[8 * g : 8 * g + 8, :], 16 * g, 1)
-    sum_out[:8, :] = packed
+    pack[:, :32] = pack[:, :32] + inner(slice(LOCAL, WIDE))
+    sum_out[:8, :] = gathered(6, 16)
     reduce_cols()
-    leave = pltpu.make_async_copy(image, w_hbm, out_sem)
+    leave = pltpu.make_async_copy(zp, z_hbm, out_sem)
     leave.start()
 
     for d, (exists, _, _, _) in enumerate(neighbours):
@@ -440,17 +430,10 @@
 
 
 def finish_kernel(
-    fem_hbm, bem_hbm, w_hbm, sums, next_fem, next_bem, hess, rfac,
-    basis, image, pack_q, pack, fem_out, bem_out, in_sem, out_sem,
+    z_hbm, sums, next_fem, next_bem, hess, rfac,
+    zp, pack_q, pack, wide, fem_out, bem_out, in_sem, out_sem,
 ):
-    copies = []
-    for b in range(2):
-        for p in range(2):
-            rows = pl.ds(b * 16, 16)
-            copies.append((fem_hbm.at[b, :, p, :], basis.at[p, rows, pl.ds(0, LOCAL)]))
-            copies.append((bem_hbm.at[b, :, p, :], basis.at[p, rows, pl.ds(LOCAL, PIECE)]))
-    copies.append((w_hbm, image))
-    copies = [pltpu.make_async_copy(a, b, in_sem.at[i]) for i, (a, b) in enumerate(copies)]
+    copies = [pltpu.make_async_copy(z_hbm.at[p], zp.at[p], in_sem.at[p]) for p in range(2)]
     for copy in copies:
         copy.start()
 
@@ -468,38 +451,45 @@
     hess[...] = both
     left = small_dot(gram_q, both, ((1,), (0,))) - one
     gram = norm + small_dot(both, left, ((0,), (0,))) - small_dot(one, both, ((0,), (0,)))
-    row_id = lax.broadcasted_iota(jnp.int32, (16, 16), 0)
-    col_id = lax.broadcasted_iota(jnp.int32, (16, 16), 1)
-    work = (gram + gram.T) * 0.5
-    inverse = (row_id == col_id).astype(F32)
-    upper = jnp.zeros((16, 16), F32)
-    lower_inv = jnp.zeros((16, 16), F32)
-    for j in range(16):
-        pivot = work[j : j + 1, j : j + 1]
-        root = lax.rsqrt(pivot)
-        root = root * (1.5 - 0.5 * pivot * root * root)
-        line = jnp.broadcast_to(work[j : j + 1, :] * root, (16, 16))
-        line_inv = jnp.broadcast_to(inverse[j : j + 1, :] * root, (16, 16))
-        column = jnp.broadcast_to(work[:, j : j + 1] * root, (16, 16))
-        upper = jnp.where((row_id == j) & (col_id >= j), line, upper)
-        lower_inv = jnp.where(row_id == j, line_inv, lower_inv)
-        work = work - column * line
-        inverse = inverse - column * line_inv
-    rfac[...] = upper
+    row_id = lax.broadcasted_iota(jnp.int32, (16, 128), 0)
+    col_id = lax.broadcasted_iota(jnp.int32, (16, 128), 1)
+    wide[...] = (col_id == row_id + 16).astype(F32)
+    wide[:, :16] = (gram + gram.T) * 0.5
+    work = wide[...]
+    rows = jnp.zeros((16, 128), F32)
+    for j in range(0, 16, 2):
+        line_a = jnp.broadcast_to(work[j : j + 1, :], (16, 128))
+        line_b = jnp.broadcast_to(work[j + 1 : j + 2, :], (16, 128))
+        col_a = jnp.broadcast_to(work[:, j : j + 1], (16, 128))
+        col_b = jnp.broadcast_to(work[:, j + 1 : j + 2], (16, 128))
+        aa = jnp.broadcast_to(col_a[j : j + 1, :], (16, 128))
+        ab = jnp.broadcast_to(col_b[j : j + 1, :], (16, 128))
+        bb = jnp.broadcast_to(col_b[j + 1 : j + 2, :], (16, 128))
+        second = line_b - line_a * (ab / aa)
+        rows = jnp.where(row_id == j, line_a, jnp.where(row_id == j + 1, second, rows))
+        if j < 14:
+            scale = 1.0 / (bb - ab * (ab / aa))
+            step = (col_b - col_a * (ab / aa)) * scale
+            work = work - col_a * (line_a / aa) - step * second
+    pivot = jnp.sum(jnp.where(row_id == col_id, rows, 0.0), axis=1, keepdims=True)
+    root = lax.rsqrt(pivot)
+    root = root * (1.5 - 0.5 * pivot * root * root)
+    rows = rows * root
+    wide[...] = jnp.where(row_id <= col_id, rows, 0.0)
+    rfac[...] = wide[:, :16]
+    wide[...] = pltpu.roll(rows, 112, 1)
+    lower_inv = wide[:, :16]
 
     weights = -small_dot(lower_inv, both, ((1,), (1,)))
     w_pair = jnp.concatenate(split2(weights), axis=0)
     l_pair = jnp.concatenate(split2(lower_inv), axis=0)
-    for copy in copies:
-        copy.wait()
     leaving = []
     for p in range(2):
-        q_high, q_low = split2(basis[p])
-        i_high, i_low = split2(image[p * 16 : p * 16 + 16, :])
-        first = jnp.dot(w_pair, q_high, preferred_element_type=F32)
-        first = first + jnp.dot(l_pair, i_high, preferred_element_type=F32)
-        second = jnp.dot(w_pair[:16], q_low, preferred_element_type=F32)
-        second = second + jnp.dot(l_pair[:16], i_low, preferred_element_type=F32)
+        copies[p].wait()
+        first = jnp.dot(w_pair, zp[p, :32, :], preferred_element_type=F32)
+        first = first + jnp.dot(l_pair, zp[p, 32:48, :], preferred_element_type=F32)
+        second = jnp.dot(w_pair[:16], zp[p, 48:80, :], preferred_element_type=F32)
+        second = second + jnp.dot(l_pair[:16], zp[p, 80:, :], preferred_element_type=F32)
         made = first[:16] + first[16:] + second
         fem_out[p] = made[:, :LOCAL]
         bem_out[p] = made[:, LOCAL:]
@@ -517,10 +507,10 @@
     vmem = pl.BlockSpec(memory_space=pltpu.VMEM)
     hbm = pl.BlockSpec(memory_space=pl.ANY)
     dma = pltpu.SemaphoreType.DMA
-    image, sums = pl.pallas_call(
+    halves, sums = pl.pallas_call(
         step_kernel,
         out_shape=(
-            jax.ShapeDtypeStruct((VEC, WIDE), F32),
+            jax.ShapeDtypeStruct((2, 96, WIDE), BF16),
             jax.ShapeDtypeStruct((16, 128), F32),
         ),
         in_specs=[hbm] * 9,
@@ -548,7 +538,7 @@
             pltpu.VMEM((ROWS, COLS, 128), F32),
             pltpu.VMEM((ROWS, COLS, 128), F32),
             pltpu.VMEM((2, 2048, 1024), BF16),
-            pltpu.VMEM((VEC, WIDE), F32),
+            pltpu.VMEM((VEC, LOCAL), F32),
             pltpu.VMEM((2, 96, WIDE), BF16),
             pltpu.VMEM((48, 128), F32),
             pltpu.VMEM((16, 128), F32),
@@ -572,20 +562,20 @@
             jax.ShapeDtypeStruct((VEC, 16), F32),
             jax.ShapeDtypeStruct((16, 16), F32),
         ),
-        in_specs=[hbm, hbm, hbm, vmem],
+        in_specs=[hbm, vmem],
         out_specs=(hbm, hbm, vmem, vmem),
         scratch_shapes=[
-            pltpu.VMEM((2, VEC, WIDE), F32),
-            pltpu.VMEM((VEC, WIDE), F32),
+            pltpu.VMEM((2, 96, WIDE), BF16),
             pltpu.VMEM((VEC, 128), F32),
             pltpu.VMEM((48, 128), F32),
+            pltpu.VMEM((16, 128), F32),
             pltpu.VMEM((2, 16, LOCAL), F32),
             pltpu.VMEM((2, 16, PIECE), F32),
-            dma((9,)),
+            dma((2,)),
             dma((4,)),
         ],
         compiler_params=pltpu.CompilerParams(vmem_limit_bytes=60 << 20),
-    )(fem_basis, bem_basis, image, sums)
+    )(halves, sums)
     return next_fem, next_bem, hess.reshape(2, 16, 16), rfac
 
 

time: 37.8 us -> 36.9 us (0.976)
  Pallas kernels: 37 us -> 36.1 us
    pallas_call x1, Pallas kernels: 32.1 us -> 31.3 us  [body(): pl.pallas_call(step_kernel, out_shape=(jax.ShapeDtypeStruct((2, 96, WIDE)...]
where the time goes in v4:
time: 36.9 us; the launch traced here: 36.8 us
  Pallas kernels  36.1 us (98%)
  between operations  0.64 us (2%)
    pallas_call x1, Pallas kernels, body(): pl.pallas_call(step_kernel, out_shape=(jax.ShapeDtypeStruct((2, 96, WIDE)...  31.3 us
    pallas_call x1, Pallas kernels, body(): pl.pallas_call(finish_kernel, out_shape=(jax.ShapeDtypeStruct((16, 2, LOC...  4.82 us

profile of v4, /device:TPU:1, one launch (start us, length us, event | category | flops | bytes accessed | tf_op | source)
XLA Modules:
  0.0 36.8 jit_solution(10770332440127974643)
XLA Ops:
  0.6 31.3 %shard_map.120 = (bf16[2,96,2176]{2,1,0:T(8,128)(2,1)}, f32[16,128]{1,0:T(8,128)}) custom-call(f32[2,16,2,2048]{3,2,1,0:T(2,128)} %fem_hbm.1, f32[2,16,2,128]{3,2,1,0:T(2,128)} %bem_hbm.1, f32[1,2048]{1,0:T(1,128)} %bitcast.4, f32[16,2048]{1,0:T(8,128)} %vals_hbm.1, s32[16,2048]{1,0:T(8,128)} %cols_hbm.1, s32[4,128]{1,0:T(4,128)} %halo_hbm.1, ...), custom_call_target="tpu_custom_call" | custom-call | tf_op jit(solution)/shard_map/pallas_call | solution.py:510
  31.9 4.8 %shard_map.121 = (f32[16,2,2048]{2,1,0:T(2,128)}, f32[16,2,128]{2,1,0:T(2,128)}, f32[32,16]{1,0:T(8,128)}, f32[16,16]{1,0:T(8,128)}) custom-call(bf16[2,96,2176]{2,1,0:T(8,128)(2,1)} %get-tuple-element.10.z_hbm, f32[16,128]{1,0:T(8,128)} %get-tuple-element.11.sums), custom_call_target="tpu_custom_call" | custom-call | tf_op jit(solution)/shard_map/pallas_call | solution.py:557

commit v5 on v4

--- a/solution.py
+++ b/solution.py
@@ -22,7 +22,7 @@
 BY_LANE_NEAR = (1, 3, 5, 7, 9, 11, 13, 15)
 BY_LANE_FAR = (1, 3, 5, 7, 9, 11, 13, 15)
 BY_LANE_ALL = (1, 3, 5, 7, 9, 11, 13, 15)
-FIRST_CHUNKS = 4
+FIRST_CHUNKS = 5
 FAR_FIRST = (
     (2, 2), (2, 1), (2, 3), (1, 2), (3, 2), (2, 0), (0, 2), (1, 1), (1, 3), (3, 1), (3, 3),
     (1, 0), (3, 0), (0, 1), (0, 3),
@@ -186,26 +186,6 @@
         @pl.when(missing)
         def _(d=d):
             halo_in[d] = jnp.zeros((VEC, 128), F32)
-
-    pl.semaphore_wait(barrier, ROWS + COLS - 2)
-
-    for k in ROW_STEPS:
-        other = lax.rem(r + k, ROWS)
-        remote(phi.at[:, mine], phi.at[:, mine], phi_send, phi_recv, other, c).start()
-
-    neighbours = (
-        (c + 1 < COLS, r, c + 1, c > 0),
-        (c > 0, r, c - 1, c + 1 < COLS),
-        (r + 1 < ROWS, r + 1, c, r > 0),
-        (r > 0, r - 1, c, r + 1 < ROWS),
-    )
-    for d, (exists, row, col, _) in enumerate(neighbours):
-
-        @pl.when(exists)
-        def _(d=d, row=row, col=col):
-            remote(
-                halo_out.at[d], halo_in.at[d], halo_send.at[d], halo_recv.at[d], row, col
-            ).start()
 
     lane = lax.broadcasted_iota(jnp.int32, (8, 128), 1)
     trace_lo = jnp.broadcast_to(trace[:, :128], (8, 128))
@@ -224,6 +204,26 @@
     )
     back = back[:VEC] + back[VEC : 2 * VEC] + back[2 * VEC :]
     swap_out[...] = jnp.concatenate(leaving + [back[:, :128], back[:, 128:]], axis=0).T
+
+    pl.semaphore_wait(barrier, ROWS + COLS - 2)
+
+    for k in ROW_STEPS:
+        other = lax.rem(r + k, ROWS)
+        remote(phi.at[:, mine], phi.at[:, mine], phi_send, phi_recv, other, c).start()
+
+    neighbours = (
+        (c + 1 < COLS, r, c + 1, c > 0),
+        (c > 0, r, c - 1, c + 1 < COLS),
+        (r + 1 < ROWS, r + 1, c, r > 0),
+        (r > 0, r - 1, c, r + 1 < ROWS),
+    )
+    for d, (exists, row, col, _) in enumerate(neighbours):
+
+        @pl.when(exists)
+        def _(d=d, row=row, col=col):
+            remote(
+                halo_out.at[d], halo_in.at[d], halo_send.at[d], halo_recv.at[d], row, col
+            ).start()
 
     for k in ROW_STEPS:
         other = lax.rem(r + k, ROWS)

time: 36.9 us -> 36.7 us (level)
  no operation moved by 1% of the time
where the time goes in v5:
time: 36.7 us; the launch traced here: 36.5 us
  Pallas kernels  35.9 us (98%)
  between operations  0.64 us (2%)
    pallas_call x1, Pallas kernels, body(): pl.pallas_call(step_kernel, out_shape=(jax.ShapeDtypeStruct((2, 96, WIDE)...  31 us
    pallas_call x1, Pallas kernels, body(): pl.pallas_call(finish_kernel, out_shape=(jax.ShapeDtypeStruct((16, 2, LOC...  4.82 us

profile of v5, /device:TPU:1, one launch (start us, length us, event | category | flops | bytes accessed | tf_op | source)
XLA Modules:
  0.0 36.5 jit_solution(2186752644541828915)
XLA Ops:
  0.6 31.0 %shard_map.120 = (bf16[2,96,2176]{2,1,0:T(8,128)(2,1)}, f32[16,128]{1,0:T(8,128)}) custom-call(f32[2,16,2,2048]{3,2,1,0:T(2,128)} %fem_hbm.1, f32[2,16,2,128]{3,2,1,0:T(2,128)} %bem_hbm.1, f32[1,2048]{1,0:T(1,128)} %bitcast.4, f32[16,2048]{1,0:T(8,128)} %vals_hbm.1, s32[16,2048]{1,0:T(8,128)} %cols_hbm.1, s32[4,128]{1,0:T(4,128)} %halo_hbm.1, ...), custom_call_target="tpu_custom_call" | custom-call | tf_op jit(solution)/shard_map/pallas_call | solution.py:510
  31.7 4.8 %shard_map.121 = (f32[16,2,2048]{2,1,0:T(2,128)}, f32[16,2,128]{2,1,0:T(2,128)}, f32[32,16]{1,0:T(8,128)}, f32[16,16]{1,0:T(8,128)}) custom-call(bf16[2,96,2176]{2,1,0:T(8,128)(2,1)} %get-tuple-element.10.z_hbm, f32[16,128]{1,0:T(8,128)} %get-tuple-element.11.sums), custom_call_target="tpu_custom_call" | custom-call | tf_op jit(solution)/shard_map/pallas_call | solution.py:557

commit v6 on v5

--- a/solution.py
+++ b/solution.py
@@ -152,9 +152,6 @@
         rows = pl.ds(pl.multiple_of(chunk * 256, 256), 256)
         return pltpu.make_async_copy(mat.at[:, rows, :], mat_buf.at[:, rows, :], mat_sem.at[k])
 
-    for k in range(8):
-        matrix_copy(k).start()
-
     def remote(src, dst, send, recv, row, col):
         return pltpu.make_async_remote_copy(
             src_ref=src, dst_ref=dst, send_sem=send, recv_sem=recv,
@@ -165,6 +162,8 @@
         pltpu.make_async_copy(ref, ref, sem).wait()
 
     ready("bem")
+    for k in range(8):
+        matrix_copy(k).start()
     mine = pl.ds(pl.multiple_of(r * PIECE, PIECE), PIECE)
     phi[:, mine] = bem[1].astype(BF16)
 

time: 36.7 us -> 36.7 us (level)
  no operation moved by 1% of the time
where the time goes in v6:
time: 36.7 us; the launch traced here: 36.5 us
  Pallas kernels  35.9 us (98%)
  between operations  0.64 us (2%)
    pallas_call x1, Pallas kernels, body(): pl.pallas_call(step_kernel, out_shape=(jax.ShapeDtypeStruct((2, 96, WIDE)...  31 us
    pallas_call x1, Pallas kernels, body(): pl.pallas_call(finish_kernel, out_shape=(jax.ShapeDtypeStruct((16, 2, LOC...  4.82 us

profile of v6, /device:TPU:1, one launch (start us, length us, event | category | flops | bytes accessed | tf_op | source)
XLA Modules:
  0.0 36.5 jit_solution(14938044979009960872)
XLA Ops:
  0.6 31.0 %shard_map.120 = (bf16[2,96,2176]{2,1,0:T(8,128)(2,1)}, f32[16,128]{1,0:T(8,128)}) custom-call(f32[2,16,2,2048]{3,2,1,0:T(2,128)} %fem_hbm.1, f32[2,16,2,128]{3,2,1,0:T(2,128)} %bem_hbm.1, f32[1,2048]{1,0:T(1,128)} %bitcast.4, f32[16,2048]{1,0:T(8,128)} %vals_hbm.1, s32[16,2048]{1,0:T(8,128)} %cols_hbm.1, s32[4,128]{1,0:T(4,128)} %halo_hbm.1, ...), custom_call_target="tpu_custom_call" | custom-call | tf_op jit(solution)/shard_map/pallas_call | solution.py:509
  31.7 4.8 %shard_map.121 = (f32[16,2,2048]{2,1,0:T(2,128)}, f32[16,2,128]{2,1,0:T(2,128)}, f32[32,16]{1,0:T(8,128)}, f32[16,16]{1,0:T(8,128)}) custom-call(bf16[2,96,2176]{2,1,0:T(8,128)(2,1)} %get-tuple-element.10.z_hbm, f32[16,128]{1,0:T(8,128)} %get-tuple-element.11.sums), custom_call_target="tpu_custom_call" | custom-call | tf_op jit(solution)/shard_map/pallas_call | solution.py:556
